TPU v7x, 256 devices: a whole 4x4x8 slice. The times are simulated.
256 devices in a mesh: dp: 32 (over x, y, core), ctx: 8 (over z).
Axes of the slice: x: 4, y: 4, z: 8, core: 2. Of those that a mesh axis runs over, the one named last changes fastest.
Arguments:
- stream: bfloat16 [128, 7168], P('ctx', 'dp'), may hold values from -40 to 40
- query: bfloat16 [2, 64, 128, 576], P(None, 'dp'), may hold values from -80 to 80
- new_latent: bfloat16 [2, 64, 576], P(None, 'dp'), may hold values from -6 to 6
- cache: bfloat16 [64, 32768, 576], P('dp', 'ctx'), may hold values from -6 to 6
- cache_scale: float32 [64, 32768], P('dp', 'ctx'), may hold values from 0.25 to 2
- lengths: int32 [64], P('dp'), may hold values from 4096 to 32768, as said below
- absorb_value: bfloat16 [128, 512, 128], P('ctx'), may hold values from -6 to 6
- out_proj: bfloat16 [16384, 7168], P('ctx', 'dp'), may hold values from -0.046875 to 0.046875
- norm_gain: bfloat16 [7168], P('dp'), may hold values from 0.25 to 1.75
- gate_weight: bfloat16 [7168, 18432], P('dp', 'ctx'), may hold values from -0.0625 to 0.0625
- up_weight: bfloat16 [7168, 18432], P('dp', 'ctx'), may hold values from -0.0625 to 0.0625
- down_weight: bfloat16 [18432, 7168], P('ctx', 'dp'), may hold values from -0.375 to 0.375
Outputs:
- result: bfloat16 [128, 7168], P('ctx', 'dp')
Inputs may be any that keep to these rules, and one draw needn't show every extreme that they name: `lengths`: every request holds at least 4096 cached positions and some request holds exactly 32768.
All inputs are finite; a program needn't handle non-finite values.
Results may differ from a plain program's by a relative error of at most 0.022.
Values may be sent and summed in bfloat16 or wider, within the bound.
No kernel may reach another device: no remote copies, remote signals or barrier semaphores. Data moves between devices by JAX's collectives and lax.ppermute only.
A program may use at most 64 MiB of HBM per device.

v0:
```python
import jax
import jax.numpy as jnp
from jax import lax
from jax.sharding import PartitionSpec as P

D = 7168
LATENT = 512
QKHEAD = 192


NEG = -1e30
EPS = 1e-06


def combined_all(part, axis, combine):
    gathered = jax.tree.map(lambda a: lax.all_gather(a, axis), part)

    def take(source):
        return jax.tree.map(lambda a: lax.dynamic_index_in_dim(a, source, 0, False), gathered)

    return lax.fori_loop(
        1, lax.axis_size(axis), lambda source, state: combine(state, take(source)), take(0)
    )


def fold_scores(carry, scores, valid, weight, values):
    run_max, run_total, run_acc = carry
    scores = jnp.where(valid, scores, NEG)
    new_max = jnp.maximum(run_max, jnp.max(scores, axis=-1))
    factor = jnp.exp(run_max - new_max)
    probs = jnp.where(valid, jnp.exp(scores - new_max[..., None]), 0.0)
    run_total = run_total * factor + jnp.sum(probs, axis=-1)
    weighted = (probs * weight).astype(jnp.bfloat16)
    run_acc = run_acc * factor[..., None] + jnp.einsum(
        "rqt,rtc->rqc", weighted, values, preferred_element_type=jnp.float32
    )
    return (new_max, run_total, run_acc)


def combine_parts(first, second):
    top = jnp.maximum(first[0], second[0])
    scale_one = jnp.exp(first[0] - top)
    scale_two = jnp.exp(second[0] - top)
    return (
        top,
        first[1] * scale_one + second[1] * scale_two,
        first[2] * scale_one[..., None] + second[2] * scale_two[..., None],
    )


def on_device(
    stream,
    query,
    new_latent,
    cache,
    cache_scale,
    lengths,
    absorb_value,
    out_proj,
    norm_gain,
    gate_weight,
    up_weight,
    down_weight,
):
    steps, req_local, heads, width = query.shape
    rows = steps * heads
    span = cache.shape[1]
    block = min(512, span)
    blocks = span // block
    scale = QKHEAD ** (-0.5)
    ctx_id = lax.axis_index("ctx")
    base = ctx_id * span
    q_rows = query.transpose(1, 0, 2, 3).reshape(req_local, rows, width)

    def one_block(j, carry):
        start = j * block
        piece = lax.dynamic_slice_in_dim(cache, start, block, 1)
        scales = lax.dynamic_slice_in_dim(cache_scale, start, block, 1)
        scores = (
            jnp.einsum("rqk,rtk->rqt", q_rows, piece, preferred_element_type=jnp.float32)
            * scales[:, None, :]
            * scale
        )
        places = base + start + jnp.arange(block, dtype=jnp.int32)
        valid = (places[None, :] < lengths[:, None])[:, None, :]
        return fold_scores(carry, scores, valid, scales[:, None, :], piece[..., :LATENT])

    start_carry = (
        jnp.full((req_local, rows), NEG, jnp.float32),
        jnp.zeros((req_local, rows), jnp.float32),
        jnp.zeros((req_local, rows, LATENT), jnp.float32),
    )
    carry = lax.fori_loop(0, blocks, one_block, start_carry)
    fresh = new_latent.transpose(1, 0, 2)
    new_scores = (
        jnp.einsum("rqk,rnk->rqn", q_rows, fresh, preferred_element_type=jnp.float32) * scale
    )
    new_ok = (jnp.arange(steps, dtype=jnp.int32)[None, :] == 0) | (
        jnp.arange(rows, dtype=jnp.int32)[:, None] >= heads
    )
    new_ok = (new_ok & (ctx_id == 0))[None, :, :]
    run_max, run_total, run_acc = fold_scores(carry, new_scores, new_ok, 1.0, fresh[..., :LATENT])
    owned = absorb_value.shape[0]
    run_max, run_total, run_acc = combined_all((run_max, run_total, run_acc), "ctx", combine_parts)
    totals = lax.dynamic_slice_in_dim(
        run_total.reshape(req_local, steps, heads), ctx_id * owned, owned, 2
    )
    sums = lax.dynamic_slice_in_dim(
        run_acc.reshape(req_local, steps, heads, LATENT), ctx_id * owned, owned, 2
    )
    attended = (sums / totals[..., None]).astype(jnp.bfloat16)
    value = jnp.einsum(
        "rshc,hcv->rshv", attended, absorb_value, preferred_element_type=jnp.float32
    ).astype(jnp.bfloat16)
    value = value.transpose(1, 0, 2, 3).reshape(steps, req_local, owned * absorb_value.shape[2])
    partial_value = jnp.einsum(
        "srf,fd->srd",
        lax.all_gather(value, "dp", axis=1, tiled=True),
        out_proj,
        preferred_element_type=jnp.float32,
    )
    partial_value = partial_value.reshape(-1, partial_value.shape[2])
    attn = lax.psum_scatter(partial_value, "ctx", scatter_dimension=0, tiled=True)
    mid = (stream.astype(jnp.float32) + attn).astype(jnp.bfloat16)
    mid32 = mid.astype(jnp.float32)
    squares = lax.psum(jnp.sum(mid32 * mid32, axis=1), "dp")
    normed = (
        mid32 * lax.rsqrt(squares / D + EPS)[:, None] * norm_gain.astype(jnp.float32)[None, :]
    ).astype(jnp.bfloat16)
    gathered = lax.all_gather(normed, "ctx", axis=0, tiled=True)
    units = gate_weight.shape[1]
    both = lax.psum_scatter(
        jnp.concatenate(
            [
                jnp.dot(gathered, gate_weight, preferred_element_type=jnp.float32),
                jnp.dot(gathered, up_weight, preferred_element_type=jnp.float32),
            ],
            axis=1,
        ),
        "dp",
        scatter_dimension=0,
        tiled=True,
    )
    hidden = (jax.nn.silu(both[:, :units]) * both[:, units:]).astype(jnp.bfloat16)
    ffn_part = jnp.dot(
        lax.all_gather(hidden, "dp", axis=0, tiled=True),
        down_weight,
        preferred_element_type=jnp.float32,
    )
    ffn = lax.psum_scatter(ffn_part, "ctx", scatter_dimension=0, tiled=True)
    return (mid32 + ffn).astype(jnp.bfloat16)


def solution(mesh):
    return jax.shard_map(
        on_device,
        mesh=mesh,
        in_specs=(
            P("ctx", "dp"),
            P(None, "dp", None, None),
            P(None, "dp", None),
            P("dp", "ctx", None),
            P("dp", "ctx"),
            P("dp"),
            P("ctx", None, None),
            P("ctx", "dp"),
            P("dp"),
            P("dp", "ctx"),
            P("dp", "ctx"),
            P("ctx", "dp"),
        ),
        out_specs=P("ctx", "dp"),
        check_vma=False,
    )
```

profile of v0, /device:TPU:1, one launch (start us, length us, event | category | flops | bytes accessed | tf_op | source)
XLA Modules:
  0.0 510.9 jit_solution(14217583709503260988)
XLA Ops:
  8.7 58.4 %while.38 = (s32[]{:T(128)}, f32[2,256]{1,0:T(2,128)S(1)}, f32[2,256]{1,0:T(2,128)S(1)}, f32[2,256,512]{2,1,0:T(8,128)}, s32[]{:T(128)}, /*index=5*/s32[2]{0:T(1...) while((s32[]{:T(128)}, f32[2,256]{1,0:T(2,128)S(1)}, ...), condition=%wide.region_3.4_spmd.clone, body=%wide.region_0.3_spmd.clone.sunk | while | flops 574099456 | bytes 8118491 | solution.py:93
  10.1 2.2 fusion.70
  12.6 3.1 convolution_add_fusion.3
  19.6 3.4 convolution_add_fusion.3
  27.0 3.4 convolution_add_fusion.3
  34.3 3.4 convolution_add_fusion.3
  41.6 3.4 convolution_add_fusion.3
  49.0 3.4 convolution_add_fusion.3
  53.8 2.2 fusion.70
  56.3 3.4 convolution_add_fusion.3
  63.7 3.4 convolution_add_fusion.3
  68.5 2.6 convolution_add_fusion.1
  71.2 21.3 %all-gather.4 = f32[8,2,256]{2,1,0:T(2,128)S(1)} all-gather(f32[1,2,256]{2,1,0:T(2,128)S(1)} %get-tuple-element.413), channel_id=3, replica_groups=mesh['dp'=32,'ctx'=8] {'ctx'}, dimensions={0}, use_global_device_ids=true | all-gather | bytes 18432 | tf_op jit(solution)/shard_map/all_gather | solution.py:16
  92.5 18.0 %all-gather.3 = f32[8,2,256]{2,1,0:T(2,128)S(1)} all-gather(f32[1,2,256]{2,1,0:T(2,128)S(1)} %bitcast.83), channel_id=2, replica_groups=mesh['dp'=32,'ctx'=8] {'ctx'}, dimensions={0}, use_global_device_ids=true | all-gather | bytes 18432 | tf_op jit(solution)/shard_map/all_gather | solution.py:16
  110.5 59.1 %all-gather.8.cloned.1.call-done = f32[16,256,512]{2,1,0:T(8,128)} async-done(((f32[2,256,512]{2,1,0:T(8,128)}), f32[16,256,512]{2,1,0:T(8,128)}) %all-gather.8.cloned.1.call-update) | async-done | bytes 8388624 | tf_op jit(solution)/shard_map/all_gather | solution.py:16
  171.0 11.0 %while.37 = (s32[]{:T(128)}, f32[2,256]{1,0:T(2,128)S(1)}, f32[2,256]{1,0:T(2,128)S(1)}, f32[2,256,512]{2,1,0:T(8,128)S(1)}, f32[8,2,256]{2,1,0:T(2,128)S(1)}, /...) while((s32[]{:T(128)}, f32[2,256]{1,0:T(2,128)S(1)}, ...), condition=%wide.region_7.8_spmd, body=%wide.region_6.7_spmd.sunk | while | flops 789509 | bytes 3166359 | solution.py:21
  182.8 25.4 %all_gather.33 = bf16[2,64,2048]{2,0,1:T(2,128)(2,1)S(1)} all-gather(bf16[2,2,2048]{2,0,1:T(2,128)(2,1)S(1)} %bitcast.82), channel_id=1, replica_groups=mesh['dp'=32,'ctx'=8] {'dp'}, dimensions={1}, use_global_device_ids=true | all-gather | bytes 540672 | tf_op jit(solution)/shard_map/all_gather | solution.py:118
  209.4 27.3 %reduce-scatter.3.cloned.1.call-done = f32[16,224]{1,0:T(8,128)} async-done(((f32[128,224]{1,0:T(8,128)}), f32[16,224]{1,0:T(8,128)}) %reduce-scatter.3.cloned.1.call-update) | async-done | bytes 14352 | tf_op jit(solution)/shard_map/reduce_scatter | solution.py:123
  237.5 68.1 %psum.7 = f32[16]{0:T(128)S(1)} all-reduce(f32[16]{0:T(128)S(1)} %get-tuple-element.411), channel_id=1, replica_groups=mesh['dp'=32,'ctx'=8] {'dp'}, use_global_device_ids=true, to_apply=%region_10.11 | all-reduce | flops 16 | bytes 128 | tf_op jit(solution)/shard_map/psum | solution.py:126
  305.7 18.6 %all_gather.34 = bf16[128,224]{1,0:T(8,128)(2,1)S(1)} all-gather(bf16[16,224]{1,0:T(8,128)(2,1)S(1)} %fusion.38), channel_id=1, replica_groups=mesh['dp'=32,'ctx'=8] {'ctx'}, dimensions={0}, use_global_device_ids=true | all-gather | bytes 64512 | tf_op jit(solution)/shard_map/all_gather | solution.py:130
  328.5 115.8 %all-reduce.3.cloned.1.call-done = f32[128,4608]{1,0:T(8,128)} async-done(((f32[128,4608]{1,0:T(8,128)}), f32[128,4608]{1,0:T(8,128)}) %all-reduce.3.cloned.1.call-update) | async-done | bytes 2359312
  445.4 25.9 %all-gather.5 = bf16[32,4,2304]{2,1,0:T(4,128)(2,1)S(1)} all-gather(bf16[1,4,2304]{2,1,0:T(4,128)(2,1)S(1)} %fusion.35), channel_id=1, replica_groups=mesh['dp'=32,'ctx'=8] {'dp'}, dimensions={0}, use_global_device_ids=true | all-gather | bytes 608256 | tf_op jit(solution)/shard_map/all_gather | solution.py:146
  471.4 2.3 fusion.48
  473.8 29.2 %reduce-scatter.5.cloned.1.call-done = f32[16,224]{1,0:T(8,128)} async-done(((f32[128,224]{1,0:T(8,128)}), f32[16,224]{1,0:T(8,128)}) %reduce-scatter.5.cloned.1.call-update) | async-done | bytes 14352 | tf_op jit(solution)/shard_map/reduce_scatter | solution.py:150
  (133 shorter events, 51.1 us)
Async XLA Ops:
  6.5 175.7 %copy-start = (bf16[16,512,128]{2,1,0:T(8,128)(2,1)S(1)}, bf16[16,512,128]{2,1,0:T(8,128)(2,1)}, u32[]{:S(2)}) copy-start(bf16[16,512,128]{2,1,0:T(8,128)(2,1)} %param.22) | copy-start | bytes 6291460
  6.5 163.1 %all-gather.8.cloned.1.call-start = ((), (), s32[]{:S(2)}) async-start(), calls=%async_computation.4 | async-start | bytes 9437184 | tf_op jit(solution)/shard_map/all_gather | solution.py:16
  8.7 58.4 %copy-start.5 = (bf16[2,2,576]{2,1,0:T(2,128)(2,1)S(1)}, bf16[2,2,576]{2,1,0:T(2,128)(2,1)}, u32[]{:S(2)}) copy-start(bf16[2,2,576]{2,1,0:T(2,128)(2,1)} %param.18) | copy-start | bytes 13828
  71.2 165.5 %reduce-scatter.3.cloned.1.call-start = ((), (), s32[]{:S(2)}) async-start(), calls=%async_computation.2 | async-start | bytes 147456 | tf_op jit(solution)/shard_map/reduce_scatter | solution.py:123
  182.2 26.0 %copy-start.3 = (bf16[2048,224]{0,1:T(8,128)(2,1)S(1)}, bf16[2048,224]{0,1:T(8,128)(2,1)}, u32[]{:S(2)}) copy-start(bf16[2048,224]{0,1:T(8,128)(2,1)} %param.23) | copy-start | bytes 2752516
  182.2 27.2 %copy-start.6 = (bf16[224]{0:T(256)(128)(2,1)S(1)}, bf16[224]{0:T(256)(128)(2,1)}, u32[]{:S(2)}) copy-start(bf16[224]{0:T(256)(128)(2,1)} %param.24) | copy-start | bytes 1348
  182.3 54.4 %copy-start.4 = (bf16[16,224]{1,0:T(8,128)(2,1)S(1)}, bf16[16,224]{1,0:T(8,128)(2,1)}, u32[]{:S(2)}) copy-start(bf16[16,224]{1,0:T(8,128)(2,1)} %param.16) | copy-start | bytes 21508
  182.3 142.1 %copy-start.1 = (bf16[224,2304]{1,0:T(8,128)(2,1)S(1)}, bf16[224,2304]{1,0:T(8,128)(2,1)}, u32[]{:S(2)}) copy-start(bf16[224,2304]{1,0:T(8,128)(2,1)} %param.25) | copy-start | bytes 3096580
  209.3 235.0 %all-reduce.3.cloned.1.call-start = ((), (), s32[]{:S(2)}) async-start(), calls=%async_computation.5 | async-start | bytes 4718592
  305.7 19.0 %copy-start.2 = (bf16[224,2304]{1,0:T(8,128)(2,1)S(1)}, bf16[224,2304]{1,0:T(8,128)(2,1)}, u32[]{:S(2)}) copy-start(bf16[224,2304]{1,0:T(8,128)(2,1)} %param.26) | copy-start | bytes 3096580
  326.6 0.7 copy-start.7
  326.6 176.4 %reduce-scatter.5.cloned.1.call-start = ((), (), s32[]{:S(2)}) async-start(), calls=%async_computation.3 | async-start | bytes 147456 | tf_op jit(solution)/shard_map/reduce_scatter | solution.py:150
Sparse Core Ops, SparseCore 0:
  71.3 98.3 all-gather.7
  209.5 27.1 reduce-scatter.2
  326.8 117.5 all-reduce.2
  473.9 29.0 reduce-scatter.4
where the time goes:
time: 517 us; the launch traced here: 511 us
  waiting for transfers between devices  232 us (45%)
  blocking collectives  177 us (34%)
  matrix products  53.3 us (10%)
  other arithmetic  23.7 us (5%)
  between operations  13.9 us (3%)
  local copies, waits for them, and re-layouts  10.5 us (2%)
    unnamed x5, waiting for transfers between devices  116 us
    psum x1, blocking collectives, on_device(): squares = lax.psum(jnp.sum(mid32 * mid32, axis=1), 'dp')  68.1 us
    all_gather x1, waiting for transfers between devices, combined_all(): gathered = jax.tree.map(lambda a: lax.all_gather(a, axis), part)  59.1 us
    all_gather x2, blocking collectives, combined_all(): gathered = jax.tree.map(lambda a: lax.all_gather(a, axis), part)  39.3 us
    dot_general x9, matrix products, fold_scores(): jnp.einsum('rqt,rtc->rqc', weighted, values, preferred_element_type=jnp.f...  29.9 us
    reduce_scatter x1, waiting for transfers between devices, on_device(): ffn = lax.psum_scatter(ffn_part, 'ctx', scatter_dimension=0, tiled=True)  29.2 us
    reduce_scatter x1, waiting for transfers between devices, on_device(): lax.psum_scatter(partial_value, 'ctx', scatter_dimension=0, tiled=True)  27.3 us
    all_gather x1, blocking collectives, on_device(): lax.all_gather(hidden, 'dp', axis=0, tiled=True)  25.9 us
  transfers between devices with their start and end apart: 4, of which 4 were waited for; matrix products, arithmetic and copies ran while one was open for 0% of the time, Pallas kernels for 0%

commit v1 on v0

v1 whole, which is shorter than its diff:
```python
import functools

import jax
import jax.numpy as jnp
from jax import lax
from jax.experimental import pallas as pl
from jax.experimental.pallas import tpu as pltpu
from jax.sharding import PartitionSpec as P

D = 7168
LATENT = 512
QKHEAD = 192
EPS = 1e-06

SCORE = QKHEAD ** (-0.5) * 1.4426950408889634
NEG = -1e30
FLOOR = -1e29
META = 128
NT = (((1,), (1,)), ((), ()))
VMEM_BYTES = 56 * 2**20


def vmem(n):
    return [pl.BlockSpec(memory_space=pltpu.VMEM)] * n


def call(kernel, out_shape, in_specs, scratch=()):
    n_out = len(out_shape) if isinstance(out_shape, tuple) else 1
    out_specs = tuple(vmem(n_out)) if isinstance(out_shape, tuple) else vmem(1)[0]
    return pl.pallas_call(
        kernel,
        in_specs=in_specs,
        out_specs=out_specs,
        out_shape=out_shape,
        scratch_shapes=list(scratch),
        compiler_params=pltpu.CompilerParams(vmem_limit_bytes=VMEM_BYTES),
    )


def pieces(x):
    first = x.astype(jnp.bfloat16).astype(jnp.float32)
    rest = x - first
    second = rest.astype(jnp.bfloat16).astype(jnp.float32)
    return first, second, (rest - second).astype(jnp.bfloat16).astype(jnp.float32)


def in_lanes(columns, rows):
    lane = lax.broadcasted_iota(jnp.int32, (rows, META), 1)
    out = jnp.zeros((rows, META), jnp.float32)
    for i, column in enumerate(columns):
        out = jnp.where(lane == i, column, out)
    return out


def attend_kernel(
    where_ref, q_ref, new_ref, scale_ref, cache_ref, out_ref, keys, scores, sems, *, sub, cuts
):
    reqs, width, span = keys.shape
    groups = out_ref.shape[0]
    steps, heads = q_ref.shape[0], q_ref.shape[3]
    rows = steps * heads
    owned = heads // groups
    cut = span // cuts
    copies = [
        [
            pltpu.make_async_copy(
                cache_ref.at[r, :, pl.ds(i * cut, cut)],
                keys.at[r, :, pl.ds(i * cut, cut)],
                sems.at[r, i],
            )
            for i in range(cuts)
        ]
        for r in range(reqs)
    ]
    for r in range(reqs):
        for i in range(cuts):
            copies[r][i].start()

    def write(r, acc, top, total):
        meta = in_lanes(pieces(top) + pieces(total), rows).astype(jnp.bfloat16)
        acc = acc.astype(jnp.bfloat16)
        for s in range(steps):
            for g in range(groups):
                at = s * heads + g * owned
                out_ref[g, r, s, :, 0:LATENT] = acc[at : at + owned]
                out_ref[g, r, s, :, LATENT:] = meta[at : at + owned]

    for r in range(reqs):
        left = where_ref[r]

        @pl.when(left <= 0)
        def _():
            for i in range(cuts):
                copies[r][i].wait()
            write(
                r,
                jnp.zeros((rows, LATENT), jnp.float32),
                jnp.full((rows, 1), FLOOR, jnp.float32),
                jnp.zeros((rows, 1), jnp.float32),
            )

        @pl.when(left > 0)
        def _():
            q = jnp.concatenate([q_ref[s, r].T for s in range(steps)], axis=0)
            n = lax.broadcasted_iota(jnp.int32, (META, width), 0)
            fresh = jnp.zeros((META, width), jnp.float32)
            for s in range(steps):
                row = new_ref[s, r : r + 1, :].astype(jnp.float32)
                fresh = jnp.where(n == s, row, fresh)
            fresh = fresh.astype(jnp.bfloat16)
            new = lax.dot_general(q, fresh, NT, preferred_element_type=jnp.float32) * SCORE
            col = lax.broadcasted_iota(jnp.int32, (rows, META), 1)
            step = lax.broadcasted_iota(jnp.int32, (rows, META), 0) // heads
            new = jnp.where((col <= step) & (where_ref[reqs] == 0), new, NEG)
            top = jnp.maximum(new, FLOOR)
            for u in range(0, span, sub):
                if u % cut == 0:
                    copies[r][u // cut].wait()
                part = jnp.dot(q, keys[r, :, u : u + sub], preferred_element_type=jnp.float32)
                ok = lax.broadcasted_iota(jnp.int32, (1, sub), 1) + u < left
                factor = jnp.where(ok, scale_ref[r : r + 1, u : u + sub] * SCORE, 0.0)
                part = part * factor + jnp.where(ok, 0.0, NEG)
                scores[:, u : u + sub] = part
                for w in range(0, sub, META):
                    top = jnp.maximum(top, part[:, w : w + META])
            top = jnp.max(top, axis=1, keepdims=True)
            probs = jnp.exp2(new - top)
            total = probs
            acc = jnp.dot(
                probs.astype(jnp.bfloat16), fresh[:, :LATENT], preferred_element_type=jnp.float32
            )
            for u in range(0, span, sub):
                probs = jnp.exp2(scores[:, u : u + sub] - top)
                for w in range(0, sub, META):
                    total = total + probs[:, w : w + META]
                probs = (probs * scale_ref[r : r + 1, u : u + sub]).astype(jnp.bfloat16)
                acc = acc + lax.dot_general(
                    probs, keys[r, 0:LATENT, u : u + sub], NT, preferred_element_type=jnp.float32
                )
            write(r, acc, top, jnp.sum(total, axis=1, keepdims=True))


def value_kernel(part_ref, absorb_ref, out_ref):
    sources, rows, _ = part_ref.shape
    owned, _, vhead = absorb_ref.shape
    tokens = rows // owned
    half = owned // 2
    tops, totals = [], []
    for c in range(sources):
        meta = part_ref[c, :, LATENT:].astype(jnp.float32)
        tops.append(meta[:, 0:1] + meta[:, 1:2] + meta[:, 2:3])
        totals.append(meta[:, 3:4] + meta[:, 4:5] + meta[:, 5:6])
    top = functools.reduce(jnp.maximum, tops)
    total = jnp.zeros_like(top)
    acc = jnp.zeros((rows, LATENT), jnp.float32)
    for c in range(sources):
        factor = jnp.exp2(tops[c] - top)
        total = total + totals[c] * factor
        acc = acc + part_ref[c, :, :LATENT].astype(jnp.float32) * factor
    attended = (acc / total).astype(jnp.bfloat16)
    sides = []
    for side in range(2):
        cols = []
        for h in range(side * half, (side + 1) * half):
            each = jnp.dot(attended, absorb_ref[h], preferred_element_type=jnp.float32)
            cols.append(each.reshape(tokens, owned, vhead)[:, h, :])
        sides.append(jnp.concatenate(cols, axis=1))
    value = jnp.concatenate(sides, axis=0).astype(jnp.bfloat16)
    out_ref[...] = jnp.broadcast_to(value[None], out_ref.shape)


def project_kernel(value_ref, weight_ref, stream_ref, out_ref):
    holders, eight, half = value_ref.shape
    copies, _, cols = out_ref.shape
    tokens = holders * eight // 2
    x = value_ref[...].astype(jnp.float32).reshape(holders * eight, half).astype(jnp.bfloat16)
    low = lax.dot_general(x, weight_ref[:, :half], NT, preferred_element_type=jnp.float32)
    high = lax.dot_general(x, weight_ref[:, half:], NT, preferred_element_type=jnp.float32)
    both = low + jnp.concatenate([high[4:], high[:4]], axis=0)
    t = lax.broadcasted_iota(jnp.int32, (tokens, holders * eight), 0)
    k = lax.broadcasted_iota(jnp.int32, (tokens, holders * eight), 1)
    per = tokens // 2
    t_in = jnp.where(t >= per, t - per, t)
    source = 8 * (t_in // 2) + 2 * (t_in % 2) + jnp.where(t >= per, 1, 0)
    pick = jnp.where(k == source, 1.0, 0.0).astype(jnp.bfloat16)
    ordered = jnp.dot(
        pick, both.astype(jnp.bfloat16), preferred_element_type=jnp.float32
    ).astype(jnp.bfloat16)
    out_ref[:, :tokens, :] = jnp.broadcast_to(ordered[None], (copies, tokens, cols))
    stream = stream_ref[...]
    out_ref[:, tokens:, :] = jnp.broadcast_to(stream[None], (copies,) + stream.shape)


def gate_kernel(part_ref, gain_ref, gate_ref, up_ref, out_ref, mid_ref):
    sources, rows, cols = part_ref.shape
    owned = mid_ref.shape[0] // sources
    tokens = sources * owned
    chips, cores, eight, width = out_ref.shape
    half = gate_ref.shape[1] // cores
    attn = part_ref[0, :tokens, :].astype(jnp.float32)
    for c in range(1, sources):
        attn = attn + part_ref[c, :tokens, :].astype(jnp.float32)
    stream = jnp.concatenate(
        [part_ref[c, tokens:, :].astype(jnp.float32) for c in range(sources)], axis=0
    )
    mid = (stream + attn).astype(jnp.bfloat16)
    mid_ref[...] = mid
    mid = mid.astype(jnp.float32)
    squares = jnp.sum(mid * mid, axis=1, keepdims=True)
    meta = in_lanes(pieces(squares), tokens).reshape(chips, eight, META).astype(jnp.bfloat16)
    x = (mid * gain_ref[...].astype(jnp.float32)).astype(jnp.bfloat16)
    for k in range(cores):
        for i, weight in enumerate((gate_ref, up_ref)):
            y = jnp.dot(
                x, weight[:, k * half : (k + 1) * half], preferred_element_type=jnp.float32
            )
            out_ref[:, k, :, i * half : (i + 1) * half] = y.reshape(chips, eight, half).astype(
                jnp.bfloat16
            )
        out_ref[:, k, :, 2 * half :] = meta


def hidden_kernel(part_ref, out_ref):
    sources = part_ref.shape[0]
    half = out_ref.shape[2]
    both = part_ref[0].astype(jnp.float32)
    for d in range(1, sources):
        both = both + part_ref[d].astype(jnp.float32)
    squares = both[:, 2 * half : 2 * half + 1] + both[:, 2 * half + 1 : 2 * half + 2]
    squares = squares + both[:, 2 * half + 2 : 2 * half + 3]
    level = lax.rsqrt(squares / D + EPS)
    gate = both[:, :half] * level
    up = both[:, half : 2 * half] * level
    hidden = (gate / (1.0 + jnp.exp(-gate)) * up).astype(jnp.bfloat16)
    out_ref[...] = jnp.broadcast_to(hidden[None], out_ref.shape)


def down_kernel(hidden_ref, weight_ref, out_ref):
    chips, cores, eight, half = hidden_ref.shape
    total = None
    for k in range(cores):
        x = hidden_ref[:, k].astype(jnp.float32).reshape(chips * eight, half).astype(jnp.bfloat16)
        y = lax.dot_general(
            x, weight_ref[:, k * half : (k + 1) * half], NT, preferred_element_type=jnp.float32
        )
        total = y if total is None else total + y
    out_ref[...] = total.reshape(out_ref.shape).astype(jnp.bfloat16)


def finish_kernel(where_ref, part_ref, mid_ref, out_ref):
    sources, owned, _ = part_ref.shape
    total = mid_ref[pl.ds(pl.multiple_of(where_ref[0] * owned, owned), owned), :].astype(
        jnp.float32
    )
    ffn = part_ref[0].astype(jnp.float32)
    for c in range(1, sources):
        ffn = ffn + part_ref[c].astype(jnp.float32)
    out_ref[...] = (total + ffn).astype(jnp.bfloat16)


def exchange(x, axis):
    return lax.all_to_all(x, axis, 0, 0)


def on_device(
    stream,
    query,
    new_latent,
    cache,
    cache_scale,
    lengths,
    absorb_value,
    out_proj,
    norm_gain,
    gate_weight,
    up_weight,
    down_weight,
):
    steps, reqs, heads, width = query.shape
    span = cache.shape[1]
    groups = lax.axis_size("ctx")
    holders = lax.axis_size("dp")
    owned = heads // groups
    vhead = absorb_value.shape[2]
    cols = stream.shape[1]
    tokens = stream.shape[0] * groups
    units = gate_weight.shape[1]
    ctx_id = lax.axis_index("ctx").astype(jnp.int32)
    bf16 = jnp.bfloat16
    smem = pl.BlockSpec(memory_space=pltpu.SMEM)

    where = jnp.concatenate([lengths - ctx_id * span, ctx_id[None]])
    cuts = 4
    part = call(
        functools.partial(attend_kernel, sub=512, cuts=cuts),
        jax.ShapeDtypeStruct((groups, reqs, steps, owned, LATENT + META), bf16),
        [smem] + vmem(3) + [pl.BlockSpec(memory_space=pl.ANY)],
        [
            pltpu.VMEM((reqs, width, span), bf16),
            pltpu.VMEM((steps * heads, span), jnp.float32),
            pltpu.SemaphoreType.DMA((reqs, cuts)),
        ],
    )(where, query.transpose(0, 1, 3, 2), new_latent, cache_scale, cache.transpose(0, 2, 1))
    part = exchange(part.reshape(groups, reqs * steps * owned, LATENT + META), "ctx")

    value = call(
        value_kernel,
        jax.ShapeDtypeStruct((holders, 2 * steps * reqs, owned * vhead // 2), bf16),
        vmem(2),
    )(part, absorb_value)
    value = exchange(value, "dp")

    attn = call(
        project_kernel,
        jax.ShapeDtypeStruct((groups, tokens + stream.shape[0], cols), bf16),
        vmem(3),
    )(value, out_proj.T, stream)
    attn = exchange(attn, "ctx")

    both, mid = call(
        gate_kernel,
        (
            jax.ShapeDtypeStruct((holders // 2, 2, tokens * 2 // holders, units + META), bf16),
            jax.ShapeDtypeStruct((tokens, cols), bf16),
        ),
        vmem(4),
    )(attn, norm_gain.reshape(1, cols), gate_weight, up_weight)
    both = exchange(both.reshape(holders, tokens * 2 // holders, units + META), "dp")

    hidden = call(
        hidden_kernel,
        jax.ShapeDtypeStruct((holders, tokens * 2 // holders, units // 2), bf16),
        vmem(1),
    )(both)
    hidden = exchange(hidden, "dp")

    ffn = call(
        down_kernel,
        jax.ShapeDtypeStruct((groups, tokens // groups, cols), bf16),
        vmem(2),
    )(hidden.reshape(holders // 2, 2, tokens * 2 // holders, units // 2), down_weight.T)
    ffn = exchange(ffn, "ctx")

    return call(
        finish_kernel,
        jax.ShapeDtypeStruct(stream.shape, bf16),
        [smem] + vmem(2),
    )(ctx_id[None], ffn, mid)


def solution(mesh):
    return jax.shard_map(
        on_device,
        mesh=mesh,
        in_specs=(
            P("ctx", "dp"),
            P(None, "dp", None, None),
            P(None, "dp", None),
            P("dp", "ctx", None),
            P("dp", "ctx"),
            P("dp"),
            P("ctx", None, None),
            P("ctx", "dp"),
            P("dp"),
            P("dp", "ctx"),
            P("dp", "ctx"),
            P("ctx", "dp"),
        ),
        out_specs=P("ctx", "dp"),
        check_vma=False,
    )
```

time: 517 us -> 154 us (0.30); the launches traced: 511 us -> 153 us
  waiting for transfers between devices: 232 us -> 18.8 us
  blocking collectives: 177 us -> 101 us
  matrix products: 53.3 us -> 0 us
  Pallas kernels: 0 us -> 27.8 us
  other arithmetic: 23.7 us -> 1.24 us
  between operations: 13.9 us -> 0.03 us
  local copies, waits for them, and re-layouts: 10.5 us -> 1.41 us
    unnamed x5 -> x0, waiting for transfers between devices: 116 us -> none
    all_gather x5 -> x0, blocking collectives: 109 us -> none  [the longest x2 39.3 us: combined_all(): gathered = jax.tree.map(lambda a: lax.all_gather(a, axis), part)]
    all_to_all x0 -> x5, blocking collectives: none -> 101 us  [exchange(): return lax.all_to_all(x, axis, 0, 0)]
    psum x1 -> x0, blocking collectives: 68.1 us -> none  [on_device(): squares = lax.psum(jnp.sum(mid32 * mid32, axis=1), 'dp')]
    all_gather x1 -> x0, waiting for transfers between devices: 59.1 us -> none  [combined_all(): gathered = jax.tree.map(lambda a: lax.all_gather(a, axis), part)]
    reduce_scatter x2 -> x0, waiting for transfers between devices: 56.5 us -> none  [the longest x1 29.2 us: on_device(): ffn = lax.psum_scatter(ffn_part, 'ctx', scatter_dimension=0, tiled=True)]
    dot_general x23 -> x0, matrix products: 53.3 us -> none  [the longest x9 29.9 us: fold_scores(): jnp.einsum('rqt,rtc->rqc', weighted, values, preferred_element_type=jnp.f...]
    pallas_call x0 -> x7, Pallas kernels: none -> 27.8 us  [the longest x1 11.8 us: on_device(): call(functools.partial(attend_kernel, sub=512, cuts=cuts), jax.ShapeDtype...]
  transfers between devices with their start and end apart: 4 -> 1, of which waited for: 4 -> 1; matrix products, arithmetic and copies ran while one was open for 0% -> 0% of each run, Pallas kernels for 0% -> 0%
where the time goes in v1:
time: 154 us; the launch traced here: 153 us
  blocking collectives  101 us (66%)
  Pallas kernels  27.8 us (18%)
  waiting for transfers between devices  18.8 us (12%)
  starting transfers between devices  3.54 us (2%)
    all_to_all x5, blocking collectives, exchange(): return lax.all_to_all(x, axis, 0, 0)  101 us
    all_to_all x1, waiting for transfers between devices, exchange(): return lax.all_to_all(x, axis, 0, 0)  18.8 us
    pallas_call x1, Pallas kernels, on_device(): call(functools.partial(attend_kernel, sub=512, cuts=cuts), jax.ShapeDtype...  11.8 us
    all_to_all x1, starting transfers between devices, exchange(): return lax.all_to_all(x, axis, 0, 0)  3.54 us
    pallas_call x1, Pallas kernels, on_device(): call(value_kernel, jax.ShapeDtypeStruct((holders, 2 * steps * reqs, owned...  3.42 us
    pallas_call x1, Pallas kernels, on_device(): call(gate_kernel, (jax.ShapeDtypeStruct((holders // 2, 2, tokens * 2 // h...  3.33 us
  transfers between devices with their start and end apart: 1, of which 1 were waited for; matrix products, arithmetic and copies ran while one was open for 0% of the time, Pallas kernels for 0%

profile of v1, /device:TPU:1, one launch (start us, length us, event | category | flops | bytes accessed | tf_op | source)
XLA Modules:
  0.0 153.5 jit_solution(17392335566069988756)
XLA Ops:
  0.0 0.7 broadcast_subtract_fusion
  0.7 0.6 pad_add_fusion.where_ref
  1.2 11.8 %shard_map.118 = bf16[8,2,2,16,640]{4,3,2,1,0:T(8,128)(2,1)} custom-call(s32[3]{0:T(128)} %pad_add_fusion.where_ref, bf16[2,2,576,128]{3,2,1,0:T(8,128)(2,1)} %bitcast.14, bf16[2,2,576]{2,1,0:T(2,128)(2,1)} %new_ref.1, f32[2,4096]{1,0:T(2,128)} %scale_ref.1, bf16[2,576,4096]{2,1,0:T(8,128)(2,1)} %bitcast.8), custom_call_target="tpu_custom_call" | custom-call | tf_op jit(solution)/shard_map/pallas_call | solution.py:294
  13.1 28.5 %all_to_all.30.part_ref = bf16[8,64,640]{2,1,0:T(8,128)(2,1)} all-to-all(bf16[8,64,640]{2,1,0:T(8,128)(2,1)} %bitcast.9), channel_id=1, replica_groups=mesh['dp'=32,'ctx'=8] {'ctx'}, dimensions={0} | all-to-all | bytes 1310720 | tf_op jit(solution)/shard_map/all_to_all | solution.py:262
  41.6 3.4 %shard_map.119 = bf16[32,8,1024]{2,1,0:T(8,128)(2,1)} custom-call(bf16[8,64,640]{2,1,0:T(8,128)(2,1)} %all_to_all.30.part_ref, bf16[16,512,128]{2,1,0:T(8,128)(2,1)} %absorb_ref.1), custom_call_target="tpu_custom_call" | custom-call | tf_op jit(solution)/shard_map/pallas_call | solution.py:306
  45.0 0.0 copy-start.1
  45.0 19.1 %all_to_all.31.value_ref = bf16[32,8,1024]{2,1,0:T(8,128)(2,1)} all-to-all(bf16[32,8,1024]{2,1,0:T(8,128)(2,1)} %shard_map.119), channel_id=1, replica_groups=mesh['dp'=32,'ctx'=8] {'dp'}, dimensions={0} | all-to-all | bytes 1048576 | tf_op jit(solution)/shard_map/all_to_all | solution.py:262
  64.1 2.8 %shard_map.120 = bf16[8,144,224]{2,1,0:T(8,128)(2,1)} custom-call(bf16[32,8,1024]{2,1,0:T(8,128)(2,1)} %all_to_all.31.value_ref, bf16[224,2048]{1,0:T(8,128)(2,1)} %bitcast.13, bf16[16,224]{1,0:T(8,128)(2,1)} %stream_ref.1), custom_call_target="tpu_custom_call" | custom-call | tf_op jit(solution)/shard_map/pallas_call | solution.py:313
  66.9 3.5 %all-to-all-start.2 = ((bf16[8,144,224]{2,1,0:T(8,128)(2,1)}), bf16[8,144,224]{2,1,0:T(8,128)(2,1)S(1)}, u32[]{:S(2)}, u32[]{:S(2)}) async-start(bf16[8,144,224]{2,1,0:T(8,128)(2,1)} %shard_map.120), calls=%async_computation.2 | async-start | bytes 1179648 | tf_op jit(solution)/shard_map/all_to_all | solution.py:262
  70.4 0.0 copy-done.1
  70.4 0.6 reshape.13.gain_ref
  71.0 18.8 %all-to-all-done.2.part_ref = bf16[8,144,224]{2,1,0:T(8,128)(2,1)S(1)} async-done(((bf16[8,144,224]{2,1,0:T(8,128)(2,1)}), bf16[8,144,224]{2,1,0:T(8,128)(2,1)S(1)}, u32[]{:S(2)}, u32[]{:S(2)}) %all-to-all-start.2) | async-done | bytes 516128 | tf_op jit(solution)/shard_map/all_to_all | solution.py:262
  89.8 0.0 copy-start
  89.8 0.8 copy-done
  90.7 3.3 %shard_map.121 = (bf16[16,2,8,2432]{3,2,1,0:T(8,128)(2,1)}, bf16[128,224]{1,0:T(8,128)(2,1)}) custom-call(bf16[8,144,224]{2,1,0:T(8,128)(2,1)} %copy-done, bf16[1,224]{1,0:T(2,128)(2,1)} %reshape.13.gain_ref, bf16[224,2304]{1,0:T(8,128)(2,1)} %gate_ref.1, bf16[224,2304]{1,0:T(8,128)(2,1)} %up_ref.1), custom_call_target="tpu_custom_call" | custom-call | tf_op jit(solution)/shard_map/pallas_call | solution.py:320
  94.0 24.4 %all_to_all.32.part_ref = bf16[32,8,2432]{2,1,0:T(8,128)(2,1)} all-to-all(bf16[32,8,2432]{2,1,0:T(8,128)(2,1)} %bitcast.11), channel_id=1, replica_groups=mesh['dp'=32,'ctx'=8] {'dp'}, dimensions={0} | all-to-all | bytes 2490368 | tf_op jit(solution)/shard_map/all_to_all | solution.py:262
  118.4 2.4 %shard_map.122 = bf16[32,8,1152]{2,1,0:T(8,128)(2,1)} custom-call(bf16[32,8,2432]{2,1,0:T(8,128)(2,1)} %all_to_all.32.part_ref), custom_call_target="tpu_custom_call" | custom-call | tf_op jit(solution)/shard_map/pallas_call | solution.py:330
  120.8 16.9 %all_to_all.33 = bf16[32,8,1152]{2,1,0:T(8,128)(2,1)} all-to-all(bf16[32,8,1152]{2,1,0:T(8,128)(2,1)} %shard_map.122), channel_id=1, replica_groups=mesh['dp'=32,'ctx'=8] {'dp'}, dimensions={0} | all-to-all | bytes 1179648 | tf_op jit(solution)/shard_map/all_to_all | solution.py:262
  137.7 2.5 %shard_map.123 = bf16[8,16,224]{2,1,0:T(8,128)(2,1)} custom-call(bf16[16,2,8,1152]{3,2,1,0:T(8,128)(2,1)} %bitcast.10, bf16[224,2304]{1,0:T(8,128)(2,1)} %bitcast.12), custom_call_target="tpu_custom_call" | custom-call | tf_op jit(solution)/shard_map/pallas_call | solution.py:337
  140.2 11.8 %all_to_all.34.part_ref = bf16[8,16,224]{2,1,0:T(8,128)(2,1)} all-to-all(bf16[8,16,224]{2,1,0:T(8,128)(2,1)} %shard_map.123), channel_id=1, replica_groups=mesh['dp'=32,'ctx'=8] {'ctx'}, dimensions={0} | all-to-all | bytes 114688 | tf_op jit(solution)/shard_map/all_to_all | solution.py:262
  152.0 1.5 shard_map.124
Async XLA Ops:
  45.0 25.4 %copy-start.1 = (bf16[224]{0:T(256)(128)(2,1)S(1)}, bf16[224]{0:T(256)(128)(2,1)}, u32[]{:S(2)}) copy-start(bf16[224]{0:T(256)(128)(2,1)} %param.20) | copy-start | bytes 1348
  66.9 22.9 %all-to-all-start.2 = ((bf16[8,144,224]{2,1,0:T(8,128)(2,1)}), bf16[8,144,224]{2,1,0:T(8,128)(2,1)S(1)}, u32[]{:S(2)}, u32[]{:S(2)}) async-start(bf16[8,144,224]{2,1,0:T(8,128)(2,1)} %shard_map.120), calls=%async_computation.2 | async-start | bytes 1179648 | tf_op jit(solution)/shard_map/all_to_all | solution.py:262
  89.8 0.8 copy-start

commit v2 on v1

v2 whole, which is shorter than its diff:
```python
import functools

import jax
import jax.numpy as jnp
from jax import lax
from jax.experimental import pallas as pl
from jax.experimental.pallas import tpu as pltpu
from jax.sharding import PartitionSpec as P

D = 7168
LATENT = 512
QKHEAD = 192
EPS = 1e-06

SCORE = QKHEAD ** (-0.5) * 1.4426950408889634
NEG = -1e30
FLOOR = -1e29
META = 128
NT = (((1,), (1,)), ((), ()))


def vmem(n):
    return [pl.BlockSpec(memory_space=pltpu.VMEM)] * n


def call(kernel, out_shape, in_specs, scratch=(), mib=14):
    n_out = len(out_shape) if isinstance(out_shape, tuple) else 1
    out_specs = tuple(vmem(n_out)) if isinstance(out_shape, tuple) else vmem(1)[0]
    return pl.pallas_call(
        kernel,
        in_specs=in_specs,
        out_specs=out_specs,
        out_shape=out_shape,
        scratch_shapes=list(scratch),
        compiler_params=pltpu.CompilerParams(vmem_limit_bytes=mib * 2**20),
    )


def pieces(x):
    first = x.astype(jnp.bfloat16).astype(jnp.float32)
    rest = x - first
    second = rest.astype(jnp.bfloat16).astype(jnp.float32)
    return first, second, (rest - second).astype(jnp.bfloat16).astype(jnp.float32)


def in_lanes(columns, rows):
    lane = lax.broadcasted_iota(jnp.int32, (rows, META), 1)
    out = jnp.zeros((rows, META), jnp.float32)
    for i, column in enumerate(columns):
        out = jnp.where(lane == i, column, out)
    return out


def attend_kernel(
    lengths_ref, q_ref, new_ref, scale_ref, cache_ref, out_ref, keys, scores, sems, *, sub, cuts
):
    ctx_id = lax.axis_index("ctx")
    reqs, width, span = keys.shape
    groups = out_ref.shape[0]
    steps, heads = q_ref.shape[0], q_ref.shape[3]
    rows = steps * heads
    owned = heads // groups
    cut = span // cuts
    copies = [
        [
            pltpu.make_async_copy(
                cache_ref.at[r, :, pl.ds(i * cut, cut)],
                keys.at[r, :, pl.ds(i * cut, cut)],
                sems.at[r, i],
            )
            for i in range(cuts)
        ]
        for r in range(reqs)
    ]
    for r in range(reqs):
        for i in range(cuts):
            copies[r][i].start()

    def write(r, acc, top, total):
        acc = acc.astype(jnp.bfloat16)
        meta = in_lanes(pieces(top) + pieces(total), rows).T[:8].astype(jnp.bfloat16)
        for g in range(groups):
            for s in range(steps):
                at = s * heads + g * owned
                to = (r * steps + s) * owned
                out_ref[g, to : to + owned, :] = acc[at : at + owned]
            out_ref[g, reqs * steps * owned :, r * rows : (r + 1) * rows] = meta

    for r in range(reqs):
        left = lengths_ref[r] - ctx_id * span

        @pl.when(left <= 0)
        def _():
            for i in range(cuts):
                copies[r][i].wait()
            write(
                r,
                jnp.zeros((rows, LATENT), jnp.float32),
                jnp.full((rows, 1), FLOOR, jnp.float32),
                jnp.zeros((rows, 1), jnp.float32),
            )

        @pl.when(left > 0)
        def _():
            q = jnp.concatenate([q_ref[s, r].T for s in range(steps)], axis=0)
            n = lax.broadcasted_iota(jnp.int32, (META, width), 0)
            fresh = jnp.zeros((META, width), jnp.float32)
            for s in range(steps):
                row = new_ref[s, r : r + 1, :].astype(jnp.float32)
                fresh = jnp.where(n == s, row, fresh)
            fresh = fresh.astype(jnp.bfloat16)
            new = lax.dot_general(q, fresh, NT, preferred_element_type=jnp.float32) * SCORE
            col = lax.broadcasted_iota(jnp.int32, (rows, META), 1)
            step = lax.broadcasted_iota(jnp.int32, (rows, META), 0) // heads
            new = jnp.where((col <= step) & (ctx_id == 0), new, NEG)
            top = jnp.maximum(new, FLOOR)
            for u in range(0, span, sub):
                if u % cut == 0:
                    copies[r][u // cut].wait()
                part = jnp.dot(q, keys[r, :, u : u + sub], preferred_element_type=jnp.float32)
                ok = lax.broadcasted_iota(jnp.int32, (1, sub), 1) + u < left
                factor = jnp.where(ok, scale_ref[r : r + 1, u : u + sub] * SCORE, 0.0)
                part = part * factor + jnp.where(ok, 0.0, NEG)
                scores[:, u : u + sub] = part
                for w in range(0, sub, META):
                    top = jnp.maximum(top, part[:, w : w + META])
            top = jnp.max(top, axis=1, keepdims=True)
            probs = jnp.exp2(new - top)
            total = probs
            acc = jnp.dot(
                probs.astype(jnp.bfloat16), fresh[:, :LATENT], preferred_element_type=jnp.float32
            )
            for u in range(0, span, sub):
                probs = jnp.exp2(scores[:, u : u + sub] - top)
                for w in range(0, sub, META):
                    total = total + probs[:, w : w + META]
                probs = (probs * scale_ref[r : r + 1, u : u + sub]).astype(jnp.bfloat16)
                acc = acc + lax.dot_general(
                    probs, keys[r, 0:LATENT, u : u + sub], NT, preferred_element_type=jnp.float32
                )
            write(r, acc, top, jnp.sum(total, axis=1, keepdims=True))


def value_kernel(part_ref, absorb_ref, out_ref, marks):
    sources = part_ref.shape[0]
    owned, _, vhead = absorb_ref.shape
    reqs, all_rows, _ = marks.shape
    rows = part_ref.shape[1] - 8
    tokens = rows // owned
    steps = tokens // reqs
    heads = all_rows // steps
    half = owned // 2
    at = lax.axis_index("ctx") * owned
    found = []
    for r in range(reqs):
        meta = [part_ref[c, rows:, r * all_rows : (r + 1) * all_rows] for c in range(sources)]
        meta = jnp.concatenate([m.astype(jnp.float32) for m in meta], axis=0)
        marks[r] = meta.T
        for s in range(steps):
            found.append(marks[r, pl.ds(pl.multiple_of(s * heads + at, owned), owned), :])
    found = jnp.concatenate(found, axis=0)
    tops, totals = [], []
    for c in range(sources):
        i = 8 * c
        tops.append(found[:, i : i + 1] + found[:, i + 1 : i + 2] + found[:, i + 2 : i + 3])
        totals.append(found[:, i + 3 : i + 4] + found[:, i + 4 : i + 5] + found[:, i + 5 : i + 6])
    top = functools.reduce(jnp.maximum, tops)
    total = jnp.zeros_like(top)
    acc = jnp.zeros((rows, LATENT), jnp.float32)
    for c in range(sources):
        factor = jnp.exp2(tops[c] - top)
        total = total + totals[c] * factor
        acc = acc + part_ref[c, :rows, :].astype(jnp.float32) * factor
    attended = (acc / total).astype(jnp.bfloat16)
    sides = []
    for side in range(2):
        cols = []
        for h in range(side * half, (side + 1) * half):
            each = jnp.dot(attended, absorb_ref[h], preferred_element_type=jnp.float32)
            cols.append(each.reshape(tokens, owned, vhead)[:, h, :])
        sides.append(jnp.concatenate(cols, axis=1))
    value = jnp.concatenate(sides, axis=0).astype(jnp.bfloat16)
    out_ref[...] = jnp.broadcast_to(value[None], out_ref.shape)


def rows_of(x):
    x = x.astype(jnp.float32)
    return x.reshape(x.shape[0] * x.shape[1], x.shape[2]).astype(jnp.bfloat16)


def project_kernel(*refs):
    value_refs, (weight_ref, stream_ref, out_ref) = refs[:-3], refs[-3:]
    copies, cols, tokens = out_ref.shape
    owned = stream_ref.shape[0]
    per = tokens // 2
    x = jnp.concatenate([rows_of(ref[...]) for ref in value_refs], axis=0)
    half = x.shape[1]
    width = x.shape[0]
    low = lax.dot_general(weight_ref[:, :half], x, NT, preferred_element_type=jnp.float32)
    high = lax.dot_general(weight_ref[:, half:], x, NT, preferred_element_type=jnp.float32)
    both = low + pltpu.roll(high, width - 4, 1)

    def place(t):
        t_in = jnp.where(t >= per, t - per, t)
        d = t_in // 2
        if len(value_refs) == 2:
            core = lax.axis_index("dp") % 2
            first = jnp.where(d % 2 == core, 0, width // 2) + 8 * (d // 2)
        else:
            first = 8 * d
        return first + 2 * (t_in % 2) + jnp.where(t >= per, 1, 0)

    def one_hot(shape, token_dim, offset):
        t = lax.broadcasted_iota(jnp.int32, shape, token_dim) + offset
        k = lax.broadcasted_iota(jnp.int32, shape, 1 - token_dim)
        return jnp.where(k == place(t), 1.0, 0.0).astype(jnp.bfloat16)

    mine = one_hot((owned, width), 0, lax.axis_index("ctx") * owned)
    both = both + lax.dot_general(
        stream_ref[...], mine, (((0,), (0,)), ((), ())), preferred_element_type=jnp.float32
    )
    ordered = jnp.dot(
        both.astype(jnp.bfloat16),
        one_hot((width, tokens), 1, 0),
        preferred_element_type=jnp.float32,
    ).astype(jnp.bfloat16)
    out_ref[...] = jnp.broadcast_to(ordered[None], out_ref.shape)


def gate_kernel(part_ref, gain_ref, gate_ref, up_ref, send_ref, keep_ref, mid_ref, whole):
    sources, cols, tokens = part_ref.shape
    owned = mid_ref.shape[0]
    chips, eight, width = send_ref.shape
    half = gate_ref.shape[1] // 2
    mid = part_ref[0].astype(jnp.float32)
    for c in range(1, sources):
        mid = mid + part_ref[c].astype(jnp.float32)
    mid = mid.astype(jnp.bfloat16).astype(jnp.float32).T
    whole[...] = mid
    at = pl.multiple_of(lax.axis_index("ctx") * owned, owned)
    mid_ref[...] = whole[pl.ds(at, owned), :].astype(jnp.bfloat16)
    squares = pieces(jnp.sum(mid * mid, axis=1, keepdims=True))
    none = (jnp.zeros_like(squares[0]),) * 3
    x = (mid * gain_ref[...].astype(jnp.float32)).astype(jnp.bfloat16)
    core = lax.axis_index("dp") % 2
    for to_ref, k, marks in (
        (send_ref, 1 - core, squares),
        (keep_ref, core, none + squares),
    ):
        for i, weight in enumerate((gate_ref, up_ref)):
            columns = pl.ds(pl.multiple_of(k * half, META), half)
            y = jnp.dot(x, weight[:, columns], preferred_element_type=jnp.float32)
            to_ref[:, :, i * half : (i + 1) * half] = y.reshape(chips, eight, half).astype(
                to_ref.dtype
            )
        to_ref[:, :, 2 * half :] = (
            in_lanes(marks, tokens).reshape(chips, eight, META).astype(to_ref.dtype)
        )


def pair_kernel(keep_ref, got_ref, out_ref):
    out_ref[...] = (keep_ref[...] + got_ref[...].astype(jnp.float32)).astype(out_ref.dtype)


def hidden_kernel(part_ref, out_ref):
    sources = part_ref.shape[0]
    half = out_ref.shape[2]
    both = part_ref[0].astype(jnp.float32)
    for d in range(1, sources):
        both = both + part_ref[d].astype(jnp.float32)
    squares = jnp.sum(both[:, 2 * half :], axis=1, keepdims=True)
    level = lax.rsqrt(squares / D + EPS)
    gate = both[:, :half] * level
    up = both[:, half : 2 * half] * level
    hidden = (gate / (1.0 + jnp.exp(-gate)) * up).astype(jnp.bfloat16)
    out_ref[...] = jnp.broadcast_to(hidden[None], out_ref.shape)


def down_kernel(own_ref, other_ref, weight_ref, out_ref):
    half = own_ref.shape[2]
    core = lax.axis_index("dp") % 2
    total = None
    for ref, k in ((own_ref, core), (other_ref, 1 - core)):
        columns = pl.ds(pl.multiple_of(k * half, META), half)
        y = lax.dot_general(
            rows_of(ref[...]), weight_ref[:, columns], NT, preferred_element_type=jnp.float32
        )
        total = y if total is None else total + y
    out_ref[...] = total.reshape(out_ref.shape).astype(jnp.bfloat16)


def finish_kernel(part_ref, mid_ref, out_ref):
    ffn = part_ref[0].astype(jnp.float32)
    for c in range(1, part_ref.shape[0]):
        ffn = ffn + part_ref[c].astype(jnp.float32)
    out_ref[...] = (mid_ref[...].astype(jnp.float32) + ffn).astype(jnp.bfloat16)


def exchange(x, axis):
    return lax.all_to_all(x, axis, 0, 0)


def exchange_chips(x):
    size = lax.axis_size("dp")
    groups = [list(range(core, size, 2)) for core in range(2)]
    return lax.all_to_all(x, "dp", 0, 0, axis_index_groups=groups)


def other_core(x):
    return lax.ppermute(x, "dp", [(i, i ^ 1) for i in range(lax.axis_size("dp"))])


def on_device(
    stream,
    query,
    new_latent,
    cache,
    cache_scale,
    lengths,
    absorb_value,
    out_proj,
    norm_gain,
    gate_weight,
    up_weight,
    down_weight,
):
    steps, reqs, heads, width = query.shape
    span = cache.shape[1]
    groups = lax.axis_size("ctx")
    holders = lax.axis_size("dp")
    owned = heads // groups
    vhead = absorb_value.shape[2]
    cols = stream.shape[1]
    tokens = stream.shape[0] * groups
    units = gate_weight.shape[1]
    chips = holders // 2
    eight = 2 * steps * reqs
    bf16 = jnp.bfloat16
    f32 = jnp.float32
    smem = pl.BlockSpec(memory_space=pltpu.SMEM)

    cuts = 4
    part = call(
        functools.partial(attend_kernel, sub=512, cuts=cuts),
        jax.ShapeDtypeStruct((groups, reqs * steps * owned + 8, LATENT), bf16),
        [smem] + vmem(3) + [pl.BlockSpec(memory_space=pltpu.HBM)],
        [
            pltpu.VMEM((reqs, width, span), bf16),
            pltpu.VMEM((steps * heads, span), f32),
            pltpu.SemaphoreType.DMA((reqs, cuts)),
        ],
        mib=56,
    )(lengths, query.transpose(0, 1, 3, 2), new_latent, cache_scale, cache.transpose(0, 2, 1))
    part = exchange(part, "ctx")

    value = call(
        value_kernel,
        jax.ShapeDtypeStruct((chips, eight, owned * vhead // 2), bf16),
        vmem(2),
        [pltpu.VMEM((reqs, steps * heads, 8 * groups), f32)],
    )(part, absorb_value)
    value = exchange_chips(value)
    value = (value, other_core(value))

    attn = call(
        project_kernel,
        jax.ShapeDtypeStruct((groups, cols, tokens), bf16),
        vmem(len(value) + 2),
    )(*value, out_proj.T, stream)
    attn = exchange(attn, "ctx")

    block = (chips, tokens // chips, units + META)
    send, keep, mid = call(
        gate_kernel,
        (
            jax.ShapeDtypeStruct(block, bf16),
            jax.ShapeDtypeStruct(block, f32),
            jax.ShapeDtypeStruct(stream.shape, bf16),
        ),
        vmem(4),
        [pltpu.VMEM((tokens, cols), f32)],
    )(attn, norm_gain.reshape(1, cols), gate_weight, up_weight)
    both = call(pair_kernel, jax.ShapeDtypeStruct(block, bf16), vmem(2))(keep, other_core(send))
    both = exchange_chips(both)

    hidden = call(
        hidden_kernel,
        jax.ShapeDtypeStruct((chips, tokens // chips, units // 2), bf16),
        vmem(1),
    )(both)
    hidden = exchange_chips(hidden)

    ffn = call(
        down_kernel,
        jax.ShapeDtypeStruct((groups, tokens // groups, cols), bf16),
        vmem(3),
    )(hidden, other_core(hidden), down_weight.T)
    ffn = exchange(ffn, "ctx")

    return call(finish_kernel, jax.ShapeDtypeStruct(stream.shape, bf16), vmem(2))(ffn, mid)


def solution(mesh):
    return jax.shard_map(
        on_device,
        mesh=mesh,
        in_specs=(
            P("ctx", "dp"),
            P(None, "dp", None, None),
            P(None, "dp", None),
            P("dp", "ctx", None),
            P("dp", "ctx"),
            P("dp"),
            P("ctx", None, None),
            P("ctx", "dp"),
            P("dp"),
            P("dp", "ctx"),
            P("dp", "ctx"),
            P("ctx", "dp"),
        ),
        out_specs=P("ctx", "dp"),
        check_vma=False,
    )
```

time: 154 us -> 122 us (0.79)
  blocking collectives: 101 us -> 76.8 us
  Pallas kernels: 27.8 us -> 16.5 us
  starting transfers between devices: 3.54 us -> 8.09 us
  waiting for transfers between devices: 18.8 us -> 20.5 us
    all_to_all x5 -> x2, blocking collectives: 101 us -> 34.5 us  [exchange(): return lax.all_to_all(x, axis, 0, 0)]
    all_to_all x0 -> x3, blocking collectives: none -> 42.3 us  [exchange_chips(): return lax.all_to_all(x, 'dp', 0, 0, axis_index_groups=groups)]
    pallas_call x5 -> x6, Pallas kernels: 13.4 us -> 4.04 us  [the longest x1 1.49 us: on_device(): call(project_kernel, jax.ShapeDtypeStruct((groups, cols, tokens), bf16),...]
    ppermute x0 -> x3, starting transfers between devices: none -> 4.62 us  [other_core(): lax.ppermute(x, 'dp', [(i, i ^ 1) for i in range(lax.axis_size('dp'))])]
    ppermute x0 -> x3, waiting for transfers between devices: none -> 4.05 us  [other_core(): lax.ppermute(x, 'dp', [(i, i ^ 1) for i in range(lax.axis_size('dp'))])]
    all_to_all x1, waiting for transfers between devices: 18.8 us -> 16.5 us  [exchange(): return lax.all_to_all(x, axis, 0, 0)]
    pallas_call x1, Pallas kernels: 2.54 us -> 0.52 us  [on_device(): call(down_kernel, jax.ShapeDtypeStruct((groups, tokens // groups, cols),...]
  transfers between devices with their start and end apart: 1 -> 4, of which waited for: 1 -> 4; matrix products, arithmetic and copies ran while one was open for 0% -> 0% of each run, Pallas kernels for 0% -> 0%
where the time goes in v2:
time: 122 us
  blocking collectives  76.8 us (63%)
  waiting for transfers between devices  20.5 us (17%)
  Pallas kernels  16.5 us (14%)
  starting transfers between devices  8.09 us (7%)
    all_to_all x3, blocking collectives, exchange_chips(): return lax.all_to_all(x, 'dp', 0, 0, axis_index_groups=groups)  42.3 us
    all_to_all x2, blocking collectives, exchange(): return lax.all_to_all(x, axis, 0, 0)  34.5 us
    all_to_all x1, waiting for transfers between devices, exchange(): return lax.all_to_all(x, axis, 0, 0)  16.5 us
    pallas_call x1, Pallas kernels, on_device(): call(functools.partial(attend_kernel, sub=512, cuts=cuts), jax.ShapeDtype...  11.9 us
    ppermute x3, starting transfers between devices, other_core(): lax.ppermute(x, 'dp', [(i, i ^ 1) for i in range(lax.axis_size('dp'))])  4.62 us
    ppermute x3, waiting for transfers between devices, other_core(): lax.ppermute(x, 'dp', [(i, i ^ 1) for i in range(lax.axis_size('dp'))])  4.05 us
    all_to_all x1, starting transfers between devices, exchange(): return lax.all_to_all(x, axis, 0, 0)  3.47 us
  transfers between devices with their start and end apart: 4, of which 4 were waited for; matrix products, arithmetic and copies ran while one was open for 0% of the time, Pallas kernels for 0%

profile of v2, /device:TPU:1, one launch (start us, length us, event | category | flops | bytes accessed | tf_op | source)
XLA Modules:
  0.0 122.1 jit_solution(14603409325753245705)
XLA Ops:
  0.0 11.9 %shard_map.118 = bf16[8,72,512]{2,1,0:T(8,128)(2,1)} custom-call(s32[2]{0:T(128)} %lengths_ref.1, bf16[2,2,576,128]{3,2,1,0:T(8,128)(2,1)} %bitcast.7, bf16[2,2,576]{2,1,0:T(2,128)(2,1)} %new_ref.1, f32[2,4096]{1,0:T(2,128)} %scale_ref.1, bf16[2,576,4096]{2,1,0:T(8,128)(2,1)} %bitcast.6), custom_call_target="tpu_custom_call" | custom-call | tf_op jit(solution)/shard_map/pallas_call | solution.py:343
  12.0 0.0 copy-start.4
  12.0 0.0 copy-start.5
  12.0 25.0 %all_to_all.30.part_ref = bf16[8,72,512]{2,1,0:T(8,128)(2,1)S(1)} all-to-all(bf16[8,72,512]{2,1,0:T(8,128)(2,1)} %shard_map.118), channel_id=1, replica_groups=mesh['dp'=32,'ctx'=8] {'ctx'}, dimensions={0} | all-to-all | bytes 1179648 | tf_op jit(solution)/shard_map/all_to_all | solution.py:300
  37.0 1.1 shard_map.119
  38.1 0.0 copy-start.6
  38.1 16.7 %all_to_all.31.refs_0_ = bf16[16,8,1024]{2,1,0:T(8,128)(2,1)S(1)} all-to-all(bf16[16,8,1024]{2,1,0:T(8,128)(2,1)S(1)} %shard_map.119), channel_id=1, replica_groups={{0,16,32,48,64,80,96,112,128,144,160,176,192,208,224,240},{8,24,40,56,7..., dimensions={0} | all-to-all | bytes 524288 | tf_op jit(solution)/shard_map/all_to_all | solution.py:306
  54.8 1.1 collective-permute-start
  55.9 1.2 collective-permute-done.refs_1_
  57.1 1.5 %shard_map.120 = bf16[8,224,128]{2,1,0:T(8,128)(2,1)} custom-call(bf16[16,8,1024]{2,1,0:T(8,128)(2,1)S(1)} %all_to_all.31.refs_0_, bf16[16,8,1024]{2,1,0:T(8,128)(2,1)S(1)} %collective-permute-done.refs_1_, bf16[224,2048]{1,0:T(8,128)(2,1)S(1)} %bitcast.5, bf16[16,224]{1,0:T(8,128)(2,1)S(1)} %copy-done.5), custom_call_target="tpu_custom_call" | custom-call | tf_op jit(solution)/shard_map/pallas_call | solution.py:365
  58.6 3.5 %all-to-all-start.2 = ((bf16[8,224,128]{2,1,0:T(8,128)(2,1)}), bf16[8,224,128]{2,1,0:T(8,128)(2,1)S(1)}, u32[]{:S(2)}, u32[]{:S(2)}) async-start(bf16[8,224,128]{2,1,0:T(8,128)(2,1)} %shard_map.120), calls=%async_computation.2 | async-start | bytes 917504 | tf_op jit(solution)/shard_map/all_to_all | solution.py:300
  62.1 16.5 %all-to-all-done.2.part_ref = bf16[8,224,128]{2,1,0:T(8,128)(2,1)S(1)} async-done(((bf16[8,224,128]{2,1,0:T(8,128)(2,1)}), bf16[8,224,128]{2,1,0:T(8,128)(2,1)S(1)}, u32[]{:S(2)}, u32[]{:S(2)}) %all-to-all-start.2) | async-done | bytes 458784 | tf_op jit(solution)/shard_map/all_to_all | solution.py:300
  78.5 0.6 shard_map.121
  79.1 0.6 collective-permute-start.1
  79.7 1.7 %collective-permute-done.1.got_ref = bf16[16,8,2432]{2,1,0:T(8,128)(2,1)S(1)} collective-permute-done((bf16[16,8,2432]{2,1,0:T(8,128)(2,1)S(1)}, bf16[16,8,2432]{2,1,0:T(8,128)(2,1)S(1)}, u32[]{:S(2)}, u32[]{:S(2)}) %collective-permute-start.1) | collective-permute-done | bytes 622624 | tf_op jit(solution)/shard_map/ppermute | solution.py:310
  81.4 0.1 shard_map.122
  81.5 14.9 %all_to_all.32.part_ref = bf16[16,8,2432]{2,1,0:T(8,128)(2,1)S(1)} all-to-all(bf16[16,8,2432]{2,1,0:T(8,128)(2,1)S(1)} %shard_map.122), channel_id=1, replica_groups={{0,16,32,48,64,80,96,112,128,144,160,176,192,208,224,240},{8,24,40,56,7..., dimensions={0} | all-to-all | bytes 1245184 | tf_op jit(solution)/shard_map/all_to_all | solution.py:306
  96.3 0.1 shard_map.123
  96.5 10.8 %all_to_all.33.own_ref = bf16[16,8,1152]{2,1,0:T(8,128)(2,1)S(1)} all-to-all(bf16[16,8,1152]{2,1,0:T(8,128)(2,1)S(1)} %shard_map.123), channel_id=1, replica_groups={{0,16,32,48,64,80,96,112,128,144,160,176,192,208,224,240},{8,24,40,56,7..., dimensions={0} | all-to-all | bytes 589824 | tf_op jit(solution)/shard_map/all_to_all | solution.py:306
  107.2 3.0 %collective-permute-start.2 = (bf16[16,8,1152]{2,1,0:T(8,128)(2,1)S(1)}, bf16[16,8,1152]{2,1,0:T(8,128)(2,1)S(1)}, u32[]{:S(2)}, u32[]{:S(2)}) collective-permute-start(bf16[16,8,1152]{2,1,0:T(8,128)(2,1)S(1)} %all_to_all.33.own_ref), channel_id=1, source_target_pairs={{0,8},{8,0},{16,24},{24,16},{32,40},{40,32},{48,56},{56,48},{64,72... | collective-permute-start | bytes 884744 | tf_op jit(solution)/shard_map/ppermute | solution.py:310
  110.2 1.2 collective-permute-done.2.other_ref
  111.4 0.5 shard_map.124
  111.9 9.5 %all_to_all.34.part_ref = bf16[8,16,224]{2,1,0:T(8,128)(2,1)S(1)} all-to-all(bf16[8,16,224]{2,1,0:T(8,128)(2,1)S(1)} %shard_map.124), channel_id=1, replica_groups=mesh['dp'=32,'ctx'=8] {'ctx'}, dimensions={0} | all-to-all | bytes 114688 | tf_op jit(solution)/shard_map/all_to_all | solution.py:300
  121.4 0.6 shard_map.125
  (12 shorter events, 0.0 us)
Async XLA Ops:
  0.0 37.0 %copy-start = (bf16[16,512,128]{2,1,0:T(8,128)(2,1)S(1)}, bf16[16,512,128]{2,1,0:T(8,128)(2,1)}, u32[]{:S(2)}) copy-start(bf16[16,512,128]{2,1,0:T(8,128)(2,1)} %absorb_ref.1) | copy-start | bytes 6291460
  12.0 45.1 %copy-start.4 = (bf16[2048,224]{0,1:T(8,128)(2,1)S(1)}, bf16[2048,224]{0,1:T(8,128)(2,1)}, u32[]{:S(2)}) copy-start(bf16[2048,224]{0,1:T(8,128)(2,1)} %param.19) | copy-start | bytes 2752516
  12.0 45.1 %copy-start.5 = (bf16[16,224]{1,0:T(8,128)(2,1)S(1)}, bf16[16,224]{1,0:T(8,128)(2,1)}, u32[]{:S(2)}) copy-start(bf16[16,224]{1,0:T(8,128)(2,1)} %refs_3_.1) | copy-start | bytes 21508
  38.1 24.0 %copy-start.6 = (bf16[224]{0:T(256)(128)(2,1)S(1)}, bf16[224]{0:T(256)(128)(2,1)}, u32[]{:S(2)}) copy-start(bf16[224]{0:T(256)(128)(2,1)} %param.20) | copy-start | bytes 1348
  38.1 40.5 %copy-start.2 = (bf16[224,2304]{1,0:T(8,128)(2,1)S(1)}, bf16[224,2304]{1,0:T(8,128)(2,1)}, u32[]{:S(2)}) copy-start(bf16[224,2304]{1,0:T(8,128)(2,1)} %gate_ref.1) | copy-start | bytes 3096580
  38.1 40.4 %copy-start.3 = (bf16[224,2304]{1,0:T(8,128)(2,1)S(1)}, bf16[224,2304]{1,0:T(8,128)(2,1)}, u32[]{:S(2)}) copy-start(bf16[224,2304]{1,0:T(8,128)(2,1)} %up_ref.1) | copy-start | bytes 3096580
  54.8 2.3 %collective-permute-start = (bf16[16,8,1024]{2,1,0:T(8,128)(2,1)S(1)}, bf16[16,8,1024]{2,1,0:T(8,128)(2,1)S(1)}, u32[]{:S(2)}, u32[]{:S(2)}) collective-permute-start(bf16[16,8,1024]{2,1,0:T(8,128)(2,1)S(1)} %all_to_all.31.refs_0_), channel_id=1, source_target_pairs={{0,8},{8,0},{16,24},{24,16},{32,40},{40,32},{48,56},{56,48},{64,72... | collective-permute-start | bytes 786440 | tf_op jit(solution)/shard_map/ppermute | solution.py:310
  58.6 20.0 %all-to-all-start.2 = ((bf16[8,224,128]{2,1,0:T(8,128)(2,1)}), bf16[8,224,128]{2,1,0:T(8,128)(2,1)S(1)}, u32[]{:S(2)}, u32[]{:S(2)}) async-start(bf16[8,224,128]{2,1,0:T(8,128)(2,1)} %shard_map.120), calls=%async_computation.2 | async-start | bytes 917504 | tf_op jit(solution)/shard_map/all_to_all | solution.py:300
  79.1 2.2 %collective-permute-start.1 = (bf16[16,8,2432]{2,1,0:T(8,128)(2,1)S(1)}, bf16[16,8,2432]{2,1,0:T(8,128)(2,1)S(1)}, u32[]{:S(2)}, u32[]{:S(2)}) collective-permute-start(bf16[16,8,2432]{2,1,0:T(8,128)(2,1)S(1)} %get-tuple-element.9), channel_id=1, source_target_pairs={{0,8},{8,0},{16,24},{24,16},{32,40},{40,32},{48,56},{56,48},{64,72... | collective-permute-start | bytes 1867784 | tf_op jit(solution)/shard_map/ppermute | solution.py:310
  81.4 30.0 %copy-start.1 = (bf16[2304,224]{0,1:T(8,128)(2,1)S(1)}, bf16[2304,224]{0,1:T(8,128)(2,1)}, u32[]{:S(2)}) copy-start(bf16[2304,224]{0,1:T(8,128)(2,1)} %param.23) | copy-start | bytes 3096580
  107.2 4.2 %collective-permute-start.2 = (bf16[16,8,1152]{2,1,0:T(8,128)(2,1)S(1)}, bf16[16,8,1152]{2,1,0:T(8,128)(2,1)S(1)}, u32[]{:S(2)}, u32[]{:S(2)}) collective-permute-start(bf16[16,8,1152]{2,1,0:T(8,128)(2,1)S(1)} %all_to_all.33.own_ref), channel_id=1, source_target_pairs={{0,8},{8,0},{16,24},{24,16},{32,40},{40,32},{48,56},{56,48},{64,72... | collective-permute-start | bytes 884744 | tf_op jit(solution)/shard_map/ppermute | solution.py:310

commit v3 on v2

--- a/solution.py
+++ b/solution.py
@@ -23,7 +23,7 @@
     return [pl.BlockSpec(memory_space=pltpu.VMEM)] * n
 
 
-def call(kernel, out_shape, in_specs, scratch=(), mib=14):
+def call(kernel, out_shape, in_specs, scratch=(), mib=14, cost=None):
     n_out = len(out_shape) if isinstance(out_shape, tuple) else 1
     out_specs = tuple(vmem(n_out)) if isinstance(out_shape, tuple) else vmem(1)[0]
     return pl.pallas_call(
@@ -33,6 +33,7 @@
         out_shape=out_shape,
         scratch_shapes=list(scratch),
         compiler_params=pltpu.CompilerParams(vmem_limit_bytes=mib * 2**20),
+        cost_estimate=cost,
     )
 
 
@@ -52,33 +53,106 @@
 
 
 def attend_kernel(
-    lengths_ref, q_ref, new_ref, scale_ref, cache_ref, out_ref, keys, scores, sems, *, sub, cuts
+    lengths_ref,
+    q_hbm,
+    new_hbm,
+    scale_hbm,
+    cache_hbm,
+    out_ref,
+    keys,
+    scores,
+    q_ref,
+    new_ref,
+    scale_ref,
+    cache_sems,
+    sems,
+    *,
+    sub,
+    cuts,
 ):
-    ctx_id = lax.axis_index("ctx")
     reqs, width, span = keys.shape
     groups = out_ref.shape[0]
     steps, heads = q_ref.shape[0], q_ref.shape[3]
     rows = steps * heads
     owned = heads // groups
     cut = span // cuts
-    copies = [
-        [
-            pltpu.make_async_copy(
-                cache_ref.at[r, :, pl.ds(i * cut, cut)],
-                keys.at[r, :, pl.ds(i * cut, cut)],
-                sems.at[r, i],
-            )
-            for i in range(cuts)
-        ]
+    ctx_id = lax.axis_index("ctx")
+    cache = [
+        pltpu.make_async_copy(
+            cache_hbm.at[r, :, pl.ds(i * cut, cut)],
+            keys.at[r, :, pl.ds(i * cut, cut)],
+            cache_sems.at[r, i],
+        )
         for r in range(reqs)
+        for i in range(cuts)
     ]
-    for r in range(reqs):
-        for i in range(cuts):
-            copies[r][i].start()
-
-    def write(r, acc, top, total):
-        acc = acc.astype(jnp.bfloat16)
-        meta = in_lanes(pieces(top) + pieces(total), rows).T[:8].astype(jnp.bfloat16)
+    small = [
+        pltpu.make_async_copy(q_hbm, q_ref, sems.at[0]),
+        pltpu.make_async_copy(new_hbm, new_ref, sems.at[1]),
+        pltpu.make_async_copy(scale_hbm, scale_ref, sems.at[2]),
+    ]
+    small[0].start()
+    cache[0].start()
+    small[1].start()
+    small[2].start()
+    cache[1].start()
+    for copy in small:
+        copy.wait()
+
+    def arrive(n):
+        cache[n].wait()
+        if n + 2 < len(cache):
+            cache[n + 2].start()
+
+    left = [lengths_ref[r] - ctx_id * span for r in range(reqs)]
+    queries, fresh, new, tops, totals, sums = ([None] * reqs for _ in range(6))
+    n = lax.broadcasted_iota(jnp.int32, (META, width), 0)
+    col = lax.broadcasted_iota(jnp.int32, (rows, META), 1)
+    step = lax.broadcasted_iota(jnp.int32, (rows, META), 0) // heads
+
+    def begin(r):
+        queries[r] = jnp.concatenate([q_ref[s, r].T for s in range(steps)], axis=0)
+        tokens = jnp.zeros((META, width), jnp.float32)
+        for s in range(steps):
+            tokens = jnp.where(n == s, new_ref[s, r : r + 1, :].astype(jnp.float32), tokens)
+        fresh[r] = tokens.astype(jnp.bfloat16)
+        each = lax.dot_general(queries[r], fresh[r], NT, preferred_element_type=jnp.float32)
+        new[r] = jnp.where((col <= step) & (ctx_id == 0), each * SCORE, NEG)
+        tops[r] = jnp.maximum(new[r], FLOOR)
+
+    def score(r, u):
+        if u % cut == 0:
+            arrive(r * cuts + u // cut)
+        part = jnp.dot(queries[r], keys[r, :, u : u + sub], preferred_element_type=jnp.float32)
+        ok = lax.broadcasted_iota(jnp.int32, (1, sub), 1) + u < left[r]
+        factor = jnp.where(ok, scale_ref[r : r + 1, u : u + sub] * SCORE, 0.0)
+        part = part * factor + jnp.where(ok, 0.0, NEG)
+        scores[r, :, u : u + sub] = part
+        for w in range(0, sub, META):
+            tops[r] = jnp.maximum(tops[r], part[:, w : w + META])
+
+    def top(r):
+        tops[r] = jnp.max(tops[r], axis=1, keepdims=True)
+        totals[r] = jnp.exp2(new[r] - tops[r])
+        sums[r] = jnp.dot(
+            totals[r].astype(jnp.bfloat16),
+            fresh[r][:, :LATENT],
+            preferred_element_type=jnp.float32,
+        )
+
+    def weigh(r, u):
+        probs = jnp.exp2(scores[r, :, u : u + sub] - tops[r])
+        for w in range(0, sub, META):
+            totals[r] = totals[r] + probs[:, w : w + META]
+        probs = (probs * scale_ref[r : r + 1, u : u + sub]).astype(jnp.bfloat16)
+        sums[r] = sums[r] + lax.dot_general(
+            probs, keys[r, 0:LATENT, u : u + sub], NT, preferred_element_type=jnp.float32
+        )
+
+    def write(r):
+        acc = sums[r].astype(jnp.bfloat16)
+        total = jnp.sum(totals[r], axis=1, keepdims=True)
+        meta = in_lanes(pieces(tops[r]) + pieces(total), rows).T[:8].astype(jnp.bfloat16)
         for g in range(groups):
             for s in range(steps):
                 at = s * heads + g * owned
@@ -87,58 +161,17 @@
             out_ref[g, reqs * steps * owned :, r * rows : (r + 1) * rows] = meta
 
     for r in range(reqs):
-        left = lengths_ref[r] - ctx_id * span
-
-        @pl.when(left <= 0)
-        def _():
-            for i in range(cuts):
-                copies[r][i].wait()
-            write(
-                r,
-                jnp.zeros((rows, LATENT), jnp.float32),
-                jnp.full((rows, 1), FLOOR, jnp.float32),
-                jnp.zeros((rows, 1), jnp.float32),
-            )
-
-        @pl.when(left > 0)
-        def _():
-            q = jnp.concatenate([q_ref[s, r].T for s in range(steps)], axis=0)
-            n = lax.broadcasted_iota(jnp.int32, (META, width), 0)
-            fresh = jnp.zeros((META, width), jnp.float32)
-            for s in range(steps):
-                row = new_ref[s, r : r + 1, :].astype(jnp.float32)
-                fresh = jnp.where(n == s, row, fresh)
-            fresh = fresh.astype(jnp.bfloat16)
-            new = lax.dot_general(q, fresh, NT, preferred_element_type=jnp.float32) * SCORE
-            col = lax.broadcasted_iota(jnp.int32, (rows, META), 1)
-            step = lax.broadcasted_iota(jnp.int32, (rows, META), 0) // heads
-            new = jnp.where((col <= step) & (ctx_id == 0), new, NEG)
-            top = jnp.maximum(new, FLOOR)
-            for u in range(0, span, sub):
-                if u % cut == 0:
-                    copies[r][u // cut].wait()
-                part = jnp.dot(q, keys[r, :, u : u + sub], preferred_element_type=jnp.float32)
-                ok = lax.broadcasted_iota(jnp.int32, (1, sub), 1) + u < left
-                factor = jnp.where(ok, scale_ref[r : r + 1, u : u + sub] * SCORE, 0.0)
-                part = part * factor + jnp.where(ok, 0.0, NEG)
-                scores[:, u : u + sub] = part
-                for w in range(0, sub, META):
-                    top = jnp.maximum(top, part[:, w : w + META])
-            top = jnp.max(top, axis=1, keepdims=True)
-            probs = jnp.exp2(new - top)
-            total = probs
-            acc = jnp.dot(
-                probs.astype(jnp.bfloat16), fresh[:, :LATENT], preferred_element_type=jnp.float32
-            )
-            for u in range(0, span, sub):
-                probs = jnp.exp2(scores[:, u : u + sub] - top)
-                for w in range(0, sub, META):
-                    total = total + probs[:, w : w + META]
-                probs = (probs * scale_ref[r : r + 1, u : u + sub]).astype(jnp.bfloat16)
-                acc = acc + lax.dot_general(
-                    probs, keys[r, 0:LATENT, u : u + sub], NT, preferred_element_type=jnp.float32
-                )
-            write(r, acc, top, jnp.sum(total, axis=1, keepdims=True))
+        begin(r)
+    for r in range(reqs + 1):
+        for u in range(0, span, sub):
+            if r < reqs:
+                score(r, u)
+            if r > 0:
+                weigh(r - 1, u)
+        if r > 0:
+            write(r - 1)
+        if r < reqs:
+            top(r)
 
 
 def value_kernel(part_ref, absorb_ref, out_ref, marks):
@@ -188,26 +221,29 @@
     return x.reshape(x.shape[0] * x.shape[1], x.shape[2]).astype(jnp.bfloat16)
 
 
-def project_kernel(*refs):
-    value_refs, (weight_ref, stream_ref, out_ref) = refs[:-3], refs[-3:]
+def product(value_ref, weight_ref):
+    x = rows_of(value_ref[...])
+    half = x.shape[1]
+    low = lax.dot_general(weight_ref[:, :half], x, NT, preferred_element_type=jnp.float32)
+    high = lax.dot_general(weight_ref[:, half:], x, NT, preferred_element_type=jnp.float32)
+    return low + pltpu.roll(high, x.shape[0] - 4, 1)
+
+
+def product_kernel(value_ref, weight_ref, out_ref):
+    out_ref[...] = product(value_ref, weight_ref)
+
+
+def project_kernel(own_ref, value_ref, weight_ref, stream_ref, out_ref):
     copies, cols, tokens = out_ref.shape
     owned = stream_ref.shape[0]
     per = tokens // 2
-    x = jnp.concatenate([rows_of(ref[...]) for ref in value_refs], axis=0)
-    half = x.shape[1]
-    width = x.shape[0]
-    low = lax.dot_general(weight_ref[:, :half], x, NT, preferred_element_type=jnp.float32)
-    high = lax.dot_general(weight_ref[:, half:], x, NT, preferred_element_type=jnp.float32)
-    both = low + pltpu.roll(high, width - 4, 1)
+    width = 2 * own_ref.shape[1]
+    core = lax.axis_index("dp") % 2
 
     def place(t):
         t_in = jnp.where(t >= per, t - per, t)
         d = t_in // 2
-        if len(value_refs) == 2:
-            core = lax.axis_index("dp") % 2
-            first = jnp.where(d % 2 == core, 0, width // 2) + 8 * (d // 2)
-        else:
-            first = 8 * d
+        first = jnp.where(d % 2 == core, 0, width // 2) + 8 * (d // 2)
         return first + 2 * (t_in % 2) + jnp.where(t >= per, 1, 0)
 
     def one_hot(shape, token_dim, offset):
@@ -215,6 +251,7 @@
         k = lax.broadcasted_iota(jnp.int32, shape, 1 - token_dim)
         return jnp.where(k == place(t), 1.0, 0.0).astype(jnp.bfloat16)
 
+    both = jnp.concatenate([own_ref[...], product(value_ref, weight_ref)], axis=1)
     mine = one_hot((owned, width), 0, lax.axis_index("ctx") * owned)
     both = both + lax.dot_general(
         stream_ref[...], mine, (((0,), (0,)), ((), ())), preferred_element_type=jnp.float32
@@ -276,16 +313,23 @@
     out_ref[...] = jnp.broadcast_to(hidden[None], out_ref.shape)
 
 
-def down_kernel(own_ref, other_ref, weight_ref, out_ref):
-    half = own_ref.shape[2]
-    core = lax.axis_index("dp") % 2
-    total = None
-    for ref, k in ((own_ref, core), (other_ref, 1 - core)):
-        columns = pl.ds(pl.multiple_of(k * half, META), half)
-        y = lax.dot_general(
-            rows_of(ref[...]), weight_ref[:, columns], NT, preferred_element_type=jnp.float32
-        )
-        total = y if total is None else total + y
+def down(hidden_ref, weight_ref, k):
+    half = hidden_ref.shape[2]
+    columns = pl.ds(pl.multiple_of(k * half, META), half)
+    return lax.dot_general(
+        rows_of(hidden_ref[...]),
+        weight_ref[:, columns],
+        NT,
+        preferred_element_type=jnp.float32,
+    )
+
+
+def down_own_kernel(hidden_ref, weight_ref, out_ref):
+    out_ref[...] = down(hidden_ref, weight_ref, lax.axis_index("dp") % 2)
+
+
+def down_kernel(own_ref, hidden_ref, weight_ref, out_ref):
+    total = own_ref[...] + down(hidden_ref, weight_ref, 1 - lax.axis_index("dp") % 2)
     out_ref[...] = total.reshape(out_ref.shape).astype(jnp.bfloat16)
 
 
@@ -339,15 +383,19 @@
     f32 = jnp.float32
     smem = pl.BlockSpec(memory_space=pltpu.SMEM)
 
-    cuts = 4
+    cuts = 2
     part = call(
         functools.partial(attend_kernel, sub=512, cuts=cuts),
         jax.ShapeDtypeStruct((groups, reqs * steps * owned + 8, LATENT), bf16),
-        [smem] + vmem(3) + [pl.BlockSpec(memory_space=pltpu.HBM)],
+        [smem] + [pl.BlockSpec(memory_space=pltpu.HBM)] * 4,
         [
             pltpu.VMEM((reqs, width, span), bf16),
-            pltpu.VMEM((steps * heads, span), f32),
+            pltpu.VMEM((reqs, steps * heads, span), f32),
+            pltpu.VMEM((steps, reqs, width, heads), bf16),
+            pltpu.VMEM((steps, reqs, width), bf16),
+            pltpu.VMEM((reqs, span), f32),
             pltpu.SemaphoreType.DMA((reqs, cuts)),
+            pltpu.SemaphoreType.DMA((3,)),
         ],
         mib=56,
     )(lengths, query.transpose(0, 1, 3, 2), new_latent, cache_scale, cache.transpose(0, 2, 1))
@@ -360,13 +408,19 @@
         [pltpu.VMEM((reqs, steps * heads, 8 * groups), f32)],
     )(part, absorb_value)
     value = exchange_chips(value)
-    value = (value, other_core(value))
-
+    other = other_core(value)
+    work = pl.CostEstimate(flops=2**29, bytes_accessed=2**20, transcendentals=0)
+    attn = call(
+        product_kernel,
+        jax.ShapeDtypeStruct((cols, chips * eight), f32),
+        vmem(2),
+        cost=work,
+    )(value, out_proj.T)
     attn = call(
         project_kernel,
         jax.ShapeDtypeStruct((groups, cols, tokens), bf16),
-        vmem(len(value) + 2),
-    )(*value, out_proj.T, stream)
+        vmem(4),
+    )(attn, other, out_proj.T, stream)
     attn = exchange(attn, "ctx")
 
     block = (chips, tokens // chips, units + META)
@@ -390,11 +444,18 @@
     )(both)
     hidden = exchange_chips(hidden)
 
+    other = other_core(hidden)
+    ffn = call(
+        down_own_kernel,
+        jax.ShapeDtypeStruct((tokens, cols), f32),
+        vmem(2),
+        cost=work,
+    )(hidden, down_weight.T)
     ffn = call(
         down_kernel,
         jax.ShapeDtypeStruct((groups, tokens // groups, cols), bf16),
         vmem(3),
-    )(hidden, other_core(hidden), down_weight.T)
+    )(ffn, other, down_weight.T)
     ffn = exchange(ffn, "ctx")
 
     return call(finish_kernel, jax.ShapeDtypeStruct(stream.shape, bf16), vmem(2))(ffn, mid)

time: 122 us -> 123 us (level)
  starting transfers between devices: 8.09 us -> 10.8 us
    ppermute x3, starting transfers between devices: 4.62 us -> 7.34 us  [other_core(): lax.ppermute(x, 'dp', [(i, i ^ 1) for i in range(lax.axis_size('dp'))])]
    all_to_all x3, blocking collectives: 42.3 us -> 39.7 us  [exchange_chips(): return lax.all_to_all(x, 'dp', 0, 0, axis_index_groups=groups)]
    all_to_all x2, blocking collectives: 34.5 us -> 36.1 us  [exchange(): return lax.all_to_all(x, axis, 0, 0)]
  transfers between devices with their start and end apart: 4 -> 4, of which waited for: 4 -> 4; matrix products, arithmetic and copies ran while one was open for 0% -> 0% of each run, Pallas kernels for 0% -> 1%
where the time goes in v3:
time: 123 us; the launch traced here: 122 us
  blocking collectives  75.8 us (62%)
  waiting for transfers between devices  19.7 us (16%)
  Pallas kernels  15.8 us (13%)
  starting transfers between devices  10.8 us (9%)
    all_to_all x3, blocking collectives, exchange_chips(): return lax.all_to_all(x, 'dp', 0, 0, axis_index_groups=groups)  39.7 us
    all_to_all x2, blocking collectives, exchange(): return lax.all_to_all(x, axis, 0, 0)  36.1 us
    all_to_all x1, waiting for transfers between devices, exchange(): return lax.all_to_all(x, axis, 0, 0)  16.5 us
    pallas_call x1, Pallas kernels, on_device(): call(functools.partial(attend_kernel, sub=512, cuts=cuts), jax.ShapeDtype...  10.8 us
    ppermute x3, starting transfers between devices, other_core(): lax.ppermute(x, 'dp', [(i, i ^ 1) for i in range(lax.axis_size('dp'))])  7.34 us
    all_to_all x1, starting transfers between devices, exchange(): return lax.all_to_all(x, axis, 0, 0)  3.47 us
    ppermute x3, waiting for transfers between devices, other_core(): lax.ppermute(x, 'dp', [(i, i ^ 1) for i in range(lax.axis_size('dp'))])  3.22 us
  transfers between devices with their start and end apart: 4, of which 4 were waited for; matrix products, arithmetic and copies ran while one was open for 0% of the time, Pallas kernels for 1%

profile of v3, /device:TPU:1, one launch (start us, length us, event | category | flops | bytes accessed | tf_op | source)
XLA Modules:
  0.0 122.2 jit_solution(2394855317569441664)
XLA Ops:
  0.0 10.8 %shard_map.118 = bf16[8,72,512]{2,1,0:T(8,128)(2,1)} custom-call(s32[2]{0:T(128)} %lengths_ref.1, bf16[2,2,576,128]{3,2,1,0:T(8,128)(2,1)} %bitcast.9, bf16[2,2,576]{2,1,0:T(2,128)(2,1)} %new_hbm.1, f32[2,4096]{1,0:T(2,128)} %scale_hbm.1, bf16[2,576,4096]{2,1,0:T(8,128)(2,1)} %bitcast.8), custom_call_target="tpu_custom_call" | custom-call | tf_op jit(solution)/shard_map/pallas_call | solution.py:387
  10.8 0.0 copy-start.4
  10.8 26.6 %all_to_all.30.part_ref = bf16[8,72,512]{2,1,0:T(8,128)(2,1)S(1)} all-to-all(bf16[8,72,512]{2,1,0:T(8,128)(2,1)} %shard_map.118), channel_id=1, replica_groups=mesh['dp'=32,'ctx'=8] {'ctx'}, dimensions={0} | all-to-all | bytes 1179648 | tf_op jit(solution)/shard_map/all_to_all | solution.py:344
  37.4 1.1 shard_map.119
  38.5 13.9 %all_to_all.31.value_ref = bf16[16,8,1024]{2,1,0:T(8,128)(2,1)S(1)} all-to-all(bf16[16,8,1024]{2,1,0:T(8,128)(2,1)S(1)} %shard_map.119), channel_id=1, replica_groups={{0,16,32,48,64,80,96,112,128,144,160,176,192,208,224,240},{8,24,40,56,7..., dimensions={0} | all-to-all | bytes 524288 | tf_op jit(solution)/shard_map/all_to_all | solution.py:350
  52.4 3.8 %collective-permute-start = (bf16[16,8,1024]{2,1,0:T(8,128)(2,1)S(1)}, bf16[16,8,1024]{2,1,0:T(8,128)(2,1)S(1)}, u32[]{:S(2)}, u32[]{:S(2)}) collective-permute-start(bf16[16,8,1024]{2,1,0:T(8,128)(2,1)S(1)} %all_to_all.31.value_ref), channel_id=1, source_target_pairs={{0,8},{8,0},{16,24},{24,16},{32,40},{40,32},{48,56},{56,48},{64,72... | collective-permute-start | bytes 786440 | tf_op jit(solution)/shard_map/ppermute | solution.py:354
  56.2 0.5 shard_map.120.own_ref
  56.7 0.7 collective-permute-done.value_ref
  57.4 1.4 %shard_map.121 = bf16[8,224,128]{2,1,0:T(8,128)(2,1)} custom-call(f32[224,128]{1,0:T(8,128)S(1)} %shard_map.120.own_ref, bf16[16,8,1024]{2,1,0:T(8,128)(2,1)S(1)} %collective-permute-done.value_ref, bf16[224,2048]{1,0:T(8,128)(2,1)S(1)} %bitcast.7, bf16[16,224]{1,0:T(8,128)(2,1)S(1)} %copy-done.5), custom_call_target="tpu_custom_call" | custom-call | tf_op jit(solution)/shard_map/pallas_call | solution.py:419
  58.8 3.5 %all-to-all-start.2 = ((bf16[8,224,128]{2,1,0:T(8,128)(2,1)}), bf16[8,224,128]{2,1,0:T(8,128)(2,1)S(1)}, u32[]{:S(2)}, u32[]{:S(2)}) async-start(bf16[8,224,128]{2,1,0:T(8,128)(2,1)} %shard_map.121), calls=%async_computation.2 | async-start | bytes 917504 | tf_op jit(solution)/shard_map/all_to_all | solution.py:344
  62.3 16.5 %all-to-all-done.2.part_ref = bf16[8,224,128]{2,1,0:T(8,128)(2,1)S(1)} async-done(((bf16[8,224,128]{2,1,0:T(8,128)(2,1)}), bf16[8,224,128]{2,1,0:T(8,128)(2,1)S(1)}, u32[]{:S(2)}, u32[]{:S(2)}) %all-to-all-start.2) | async-done | bytes 458784 | tf_op jit(solution)/shard_map/all_to_all | solution.py:344
  78.7 0.6 shard_map.122
  79.3 0.6 collective-permute-start.1
  79.9 1.7 %collective-permute-done.1.got_ref = bf16[16,8,2432]{2,1,0:T(8,128)(2,1)S(1)} collective-permute-done((bf16[16,8,2432]{2,1,0:T(8,128)(2,1)S(1)}, bf16[16,8,2432]{2,1,0:T(8,128)(2,1)S(1)}, u32[]{:S(2)}, u32[]{:S(2)}) %collective-permute-start.1) | collective-permute-done | bytes 622624 | tf_op jit(solution)/shard_map/ppermute | solution.py:354
  81.6 0.1 shard_map.123
  81.7 15.0 %all_to_all.32.part_ref = bf16[16,8,2432]{2,1,0:T(8,128)(2,1)S(1)} all-to-all(bf16[16,8,2432]{2,1,0:T(8,128)(2,1)S(1)} %shard_map.123), channel_id=1, replica_groups={{0,16,32,48,64,80,96,112,128,144,160,176,192,208,224,240},{8,24,40,56,7..., dimensions={0} | all-to-all | bytes 1245184 | tf_op jit(solution)/shard_map/all_to_all | solution.py:350
  96.7 0.1 shard_map.124
  96.9 10.8 %all_to_all.33.hidden_ref = bf16[16,8,1152]{2,1,0:T(8,128)(2,1)S(1)} all-to-all(bf16[16,8,1152]{2,1,0:T(8,128)(2,1)S(1)} %shard_map.124), channel_id=1, replica_groups={{0,16,32,48,64,80,96,112,128,144,160,176,192,208,224,240},{8,24,40,56,7..., dimensions={0} | all-to-all | bytes 589824 | tf_op jit(solution)/shard_map/all_to_all | solution.py:350
  107.6 3.0 %collective-permute-start.2 = (bf16[16,8,1152]{2,1,0:T(8,128)(2,1)S(1)}, bf16[16,8,1152]{2,1,0:T(8,128)(2,1)S(1)}, u32[]{:S(2)}, u32[]{:S(2)}) collective-permute-start(bf16[16,8,1152]{2,1,0:T(8,128)(2,1)S(1)} %all_to_all.33.hidden_ref), channel_id=1, source_target_pairs={{0,8},{8,0},{16,24},{24,16},{32,40},{40,32},{48,56},{56,48},{64,72... | collective-permute-start | bytes 884744 | tf_op jit(solution)/shard_map/ppermute | solution.py:354
  110.6 0.3 shard_map.125.own_ref
  110.9 0.9 collective-permute-done.2.hidden_ref
  111.8 0.3 shard_map.126
  112.1 9.5 %all_to_all.34.part_ref = bf16[8,16,224]{2,1,0:T(8,128)(2,1)S(1)} all-to-all(bf16[8,16,224]{2,1,0:T(8,128)(2,1)S(1)} %shard_map.126), channel_id=1, replica_groups=mesh['dp'=32,'ctx'=8] {'ctx'}, dimensions={0} | all-to-all | bytes 114688 | tf_op jit(solution)/shard_map/all_to_all | solution.py:344
  121.6 0.6 shard_map.127
  (14 shorter events, 0.0 us)
Async XLA Ops:
  0.0 37.4 %copy-start = (bf16[16,512,128]{2,1,0:T(8,128)(2,1)S(1)}, bf16[16,512,128]{2,1,0:T(8,128)(2,1)}, u32[]{:S(2)}) copy-start(bf16[16,512,128]{2,1,0:T(8,128)(2,1)} %absorb_ref.1) | copy-start | bytes 6291460
  10.8 45.4 %copy-start.4 = (bf16[2048,224]{0,1:T(8,128)(2,1)S(1)}, bf16[2048,224]{0,1:T(8,128)(2,1)}, u32[]{:S(2)}) copy-start(bf16[2048,224]{0,1:T(8,128)(2,1)} %param.19) | copy-start | bytes 2752516
  37.4 20.0 %copy-start.5 = (bf16[16,224]{1,0:T(8,128)(2,1)S(1)}, bf16[16,224]{1,0:T(8,128)(2,1)}, u32[]{:S(2)}) copy-start(bf16[16,224]{1,0:T(8,128)(2,1)} %stream_ref.1) | copy-start | bytes 21508
  52.4 5.0 %collective-permute-start = (bf16[16,8,1024]{2,1,0:T(8,128)(2,1)S(1)}, bf16[16,8,1024]{2,1,0:T(8,128)(2,1)S(1)}, u32[]{:S(2)}, u32[]{:S(2)}) collective-permute-start(bf16[16,8,1024]{2,1,0:T(8,128)(2,1)S(1)} %all_to_all.31.value_ref), channel_id=1, source_target_pairs={{0,8},{8,0},{16,24},{24,16},{32,40},{40,32},{48,56},{56,48},{64,72... | collective-permute-start | bytes 786440 | tf_op jit(solution)/shard_map/ppermute | solution.py:354
  56.2 6.0 %copy-start.6 = (bf16[224]{0:T(256)(128)(2,1)S(1)}, bf16[224]{0:T(256)(128)(2,1)}, u32[]{:S(2)}) copy-start(bf16[224]{0:T(256)(128)(2,1)} %param.20) | copy-start | bytes 1348
  56.2 22.5 %copy-start.2 = (bf16[224,2304]{1,0:T(8,128)(2,1)S(1)}, bf16[224,2304]{1,0:T(8,128)(2,1)}, u32[]{:S(2)}) copy-start(bf16[224,2304]{1,0:T(8,128)(2,1)} %gate_ref.1) | copy-start | bytes 3096580
  56.2 22.5 %copy-start.3 = (bf16[224,2304]{1,0:T(8,128)(2,1)S(1)}, bf16[224,2304]{1,0:T(8,128)(2,1)}, u32[]{:S(2)}) copy-start(bf16[224,2304]{1,0:T(8,128)(2,1)} %up_ref.1) | copy-start | bytes 3096580
  58.8 20.0 %all-to-all-start.2 = ((bf16[8,224,128]{2,1,0:T(8,128)(2,1)}), bf16[8,224,128]{2,1,0:T(8,128)(2,1)S(1)}, u32[]{:S(2)}, u32[]{:S(2)}) async-start(bf16[8,224,128]{2,1,0:T(8,128)(2,1)} %shard_map.121), calls=%async_computation.2 | async-start | bytes 917504 | tf_op jit(solution)/shard_map/all_to_all | solution.py:344
  79.3 2.2 %collective-permute-start.1 = (bf16[16,8,2432]{2,1,0:T(8,128)(2,1)S(1)}, bf16[16,8,2432]{2,1,0:T(8,128)(2,1)S(1)}, u32[]{:S(2)}, u32[]{:S(2)}) collective-permute-start(bf16[16,8,2432]{2,1,0:T(8,128)(2,1)S(1)} %get-tuple-element.9), channel_id=1, source_target_pairs={{0,8},{8,0},{16,24},{24,16},{32,40},{40,32},{48,56},{56,48},{64,72... | collective-permute-start | bytes 1867784 | tf_op jit(solution)/shard_map/ppermute | solution.py:354
  81.6 29.0 %copy-start.1 = (bf16[2304,224]{0,1:T(8,128)(2,1)S(1)}, bf16[2304,224]{0,1:T(8,128)(2,1)}, u32[]{:S(2)}) copy-start(bf16[2304,224]{0,1:T(8,128)(2,1)} %param.23) | copy-start | bytes 3096580
  107.6 4.2 %collective-permute-start.2 = (bf16[16,8,1152]{2,1,0:T(8,128)(2,1)S(1)}, bf16[16,8,1152]{2,1,0:T(8,128)(2,1)S(1)}, u32[]{:S(2)}, u32[]{:S(2)}) collective-permute-start(bf16[16,8,1152]{2,1,0:T(8,128)(2,1)S(1)} %all_to_all.33.hidden_ref), channel_id=1, source_target_pairs={{0,8},{8,0},{16,24},{24,16},{32,40},{40,32},{48,56},{56,48},{64,72... | collective-permute-start | bytes 884744 | tf_op jit(solution)/shard_map/ppermute | solution.py:354

commit v4 on v3

--- a/solution.py
+++ b/solution.py
@@ -91,18 +91,6 @@
         pltpu.make_async_copy(new_hbm, new_ref, sems.at[1]),
         pltpu.make_async_copy(scale_hbm, scale_ref, sems.at[2]),
     ]
-    small[0].start()
-    cache[0].start()
-    small[1].start()
-    small[2].start()
-    cache[1].start()
-    for copy in small:
-        copy.wait()
-
-    def arrive(n):
-        cache[n].wait()
-        if n + 2 < len(cache):
-            cache[n + 2].start()
 
     left = [lengths_ref[r] - ctx_id * span for r in range(reqs)]
     queries, fresh, new, tops, totals, sums = ([None] * reqs for _ in range(6))
@@ -121,8 +109,6 @@
         tops[r] = jnp.maximum(new[r], FLOOR)
 
     def score(r, u):
-        if u % cut == 0:
-            arrive(r * cuts + u // cut)
         part = jnp.dot(queries[r], keys[r, :, u : u + sub], preferred_element_type=jnp.float32)
         ok = lax.broadcasted_iota(jnp.int32, (1, sub), 1) + u < left[r]
         factor = jnp.where(ok, scale_ref[r : r + 1, u : u + sub] * SCORE, 0.0)
@@ -160,18 +146,60 @@
                 out_ref[g, to : to + owned, :] = acc[at : at + owned]
             out_ref[g, reqs * steps * owned :, r * rows : (r + 1) * rows] = meta
 
-    for r in range(reqs):
-        begin(r)
-    for r in range(reqs + 1):
-        for u in range(0, span, sub):
-            if r < reqs:
-                score(r, u)
-            if r > 0:
-                weigh(r - 1, u)
-        if r > 0:
-            write(r - 1)
-        if r < reqs:
-            top(r)
+    def attend(active):
+        order = [r * cuts + i for r in active for i in range(cuts)]
+        small[0].start()
+        cache[order[0]].start()
+        small[1].start()
+        small[2].start()
+        cache[order[1]].start()
+        for copy in small:
+            copy.wait()
+        for r in active:
+            begin(r)
+        for n in range(len(active) + 1):
+            for u in range(0, span, sub):
+                if n < len(active):
+                    if u % cut == 0:
+                        at = n * cuts + u // cut
+                        cache[order[at]].wait()
+                        if at + 2 < len(order):
+                            cache[order[at + 2]].start()
+                    score(active[n], u)
+                if n > 0:
+                    weigh(active[n - 1], u)
+            if n > 0:
+                write(active[n - 1])
+            if n < len(active):
+                top(active[n])
+        for r in range(reqs):
+            if r not in active:
+                skip(r)
+
+    def skip(r):
+        tops[r] = jnp.full((rows, 1), FLOOR, jnp.float32)
+        totals[r] = jnp.zeros((rows, 1), jnp.float32)
+        sums[r] = jnp.zeros((rows, LATENT), jnp.float32)
+        write(r)
+
+    first, second = (left[r] > 0 for r in range(reqs))
+
+    @pl.when(first & second)
+    def _():
+        attend([0, 1])
+
+    @pl.when(first & ~second)
+    def _():
+        attend([0])
+
+    @pl.when(second & ~first)
+    def _():
+        attend([1])
+
+    @pl.when(~first & ~second)
+    def _():
+        for r in range(reqs):
+            skip(r)
 
 
 def value_kernel(part_ref, absorb_ref, out_ref, marks):

time: 123 us -> 121 us (0.984)
  starting transfers between devices: 10.8 us -> 8.92 us
    all_to_all x3, blocking collectives: 39.7 us -> 43.6 us  [exchange_chips(): return lax.all_to_all(x, 'dp', 0, 0, axis_index_groups=groups)]
    all_to_all x2, blocking collectives: 36.1 us -> 32.5 us  [exchange(): return lax.all_to_all(x, axis, 0, 0)]
    ppermute x3, starting transfers between devices: 7.34 us -> 5.45 us  [other_core(): lax.ppermute(x, 'dp', [(i, i ^ 1) for i in range(lax.axis_size('dp'))])]
where the time goes in v4:
time: 121 us
  blocking collectives  76.1 us (63%)
  waiting for transfers between devices  19.7 us (16%)
  Pallas kernels  16.1 us (13%)
  starting transfers between devices  8.92 us (7%)
    all_to_all x3, blocking collectives, exchange_chips(): return lax.all_to_all(x, 'dp', 0, 0, axis_index_groups=groups)  43.6 us
    all_to_all x2, blocking collectives, exchange(): return lax.all_to_all(x, axis, 0, 0)  32.5 us
    all_to_all x1, waiting for transfers between devices, exchange(): return lax.all_to_all(x, axis, 0, 0)  16.5 us
    pallas_call x1, Pallas kernels, on_device(): call(functools.partial(attend_kernel, sub=512, cuts=cuts), jax.ShapeDtype...  11.1 us
    ppermute x3, starting transfers between devices, other_core(): lax.ppermute(x, 'dp', [(i, i ^ 1) for i in range(lax.axis_size('dp'))])  5.45 us
    all_to_all x1, starting transfers between devices, exchange(): return lax.all_to_all(x, axis, 0, 0)  3.47 us
    ppermute x3, waiting for transfers between devices, other_core(): lax.ppermute(x, 'dp', [(i, i ^ 1) for i in range(lax.axis_size('dp'))])  3.22 us
  transfers between devices with their start and end apart: 4, of which 4 were waited for; matrix products, arithmetic and copies ran while one was open for 0% of the time, Pallas kernels for 1%

profile of v4, /device:TPU:1, one launch (start us, length us, event | category | flops | bytes accessed | tf_op | source)
XLA Modules:
  0.0 120.9 jit_solution(17813227775562282909)
XLA Ops:
  0.0 11.1 %shard_map.118 = bf16[8,72,512]{2,1,0:T(8,128)(2,1)} custom-call(s32[2]{0:T(128)} %lengths_ref.1, bf16[2,2,576,128]{3,2,1,0:T(8,128)(2,1)} %bitcast.9, bf16[2,2,576]{2,1,0:T(2,128)(2,1)} %new_hbm.1, f32[2,4096]{1,0:T(2,128)} %scale_hbm.1, bf16[2,576,4096]{2,1,0:T(8,128)(2,1)} %bitcast.8), custom_call_target="tpu_custom_call" | custom-call | tf_op jit(solution)/shard_map/pallas_call | solution.py:415
  11.1 0.0 copy-start.4
  11.1 22.9 %all_to_all.30.part_ref = bf16[8,72,512]{2,1,0:T(8,128)(2,1)S(1)} all-to-all(bf16[8,72,512]{2,1,0:T(8,128)(2,1)} %shard_map.118), channel_id=1, replica_groups=mesh['dp'=32,'ctx'=8] {'ctx'}, dimensions={0} | all-to-all | bytes 1179648 | tf_op jit(solution)/shard_map/all_to_all | solution.py:372
  34.0 1.1 shard_map.119
  35.1 17.9 %all_to_all.31.value_ref = bf16[16,8,1024]{2,1,0:T(8,128)(2,1)S(1)} all-to-all(bf16[16,8,1024]{2,1,0:T(8,128)(2,1)S(1)} %shard_map.119), channel_id=1, replica_groups={{0,16,32,48,64,80,96,112,128,144,160,176,192,208,224,240},{8,24,40,56,7..., dimensions={0} | all-to-all | bytes 524288 | tf_op jit(solution)/shard_map/all_to_all | solution.py:378
  53.0 1.9 %collective-permute-start = (bf16[16,8,1024]{2,1,0:T(8,128)(2,1)S(1)}, bf16[16,8,1024]{2,1,0:T(8,128)(2,1)S(1)}, u32[]{:S(2)}, u32[]{:S(2)}) collective-permute-start(bf16[16,8,1024]{2,1,0:T(8,128)(2,1)S(1)} %all_to_all.31.value_ref), channel_id=1, source_target_pairs={{0,8},{8,0},{16,24},{24,16},{32,40},{40,32},{48,56},{56,48},{64,72... | collective-permute-start | bytes 786440 | tf_op jit(solution)/shard_map/ppermute | solution.py:382
  54.9 0.5 shard_map.120.own_ref
  55.4 0.7 collective-permute-done.value_ref
  56.1 1.4 %shard_map.121 = bf16[8,224,128]{2,1,0:T(8,128)(2,1)} custom-call(f32[224,128]{1,0:T(8,128)S(1)} %shard_map.120.own_ref, bf16[16,8,1024]{2,1,0:T(8,128)(2,1)S(1)} %collective-permute-done.value_ref, bf16[224,2048]{1,0:T(8,128)(2,1)S(1)} %bitcast.7, bf16[16,224]{1,0:T(8,128)(2,1)S(1)} %copy-done.5), custom_call_target="tpu_custom_call" | custom-call | tf_op jit(solution)/shard_map/pallas_call | solution.py:447
  57.5 3.5 %all-to-all-start.2 = ((bf16[8,224,128]{2,1,0:T(8,128)(2,1)}), bf16[8,224,128]{2,1,0:T(8,128)(2,1)S(1)}, u32[]{:S(2)}, u32[]{:S(2)}) async-start(bf16[8,224,128]{2,1,0:T(8,128)(2,1)} %shard_map.121), calls=%async_computation.2 | async-start | bytes 917504 | tf_op jit(solution)/shard_map/all_to_all | solution.py:372
  61.0 16.5 %all-to-all-done.2.part_ref = bf16[8,224,128]{2,1,0:T(8,128)(2,1)S(1)} async-done(((bf16[8,224,128]{2,1,0:T(8,128)(2,1)}), bf16[8,224,128]{2,1,0:T(8,128)(2,1)S(1)}, u32[]{:S(2)}, u32[]{:S(2)}) %all-to-all-start.2) | async-done | bytes 458784 | tf_op jit(solution)/shard_map/all_to_all | solution.py:372
  77.5 0.6 shard_map.122
  78.1 0.6 collective-permute-start.1
  78.6 1.7 %collective-permute-done.1.got_ref = bf16[16,8,2432]{2,1,0:T(8,128)(2,1)S(1)} collective-permute-done((bf16[16,8,2432]{2,1,0:T(8,128)(2,1)S(1)}, bf16[16,8,2432]{2,1,0:T(8,128)(2,1)S(1)}, u32[]{:S(2)}, u32[]{:S(2)}) %collective-permute-start.1) | collective-permute-done | bytes 622624 | tf_op jit(solution)/shard_map/ppermute | solution.py:382
  80.3 0.1 shard_map.123
  80.4 15.0 %all_to_all.32.part_ref = bf16[16,8,2432]{2,1,0:T(8,128)(2,1)S(1)} all-to-all(bf16[16,8,2432]{2,1,0:T(8,128)(2,1)S(1)} %shard_map.123), channel_id=1, replica_groups={{0,16,32,48,64,80,96,112,128,144,160,176,192,208,224,240},{8,24,40,56,7..., dimensions={0} | all-to-all | bytes 1245184 | tf_op jit(solution)/shard_map/all_to_all | solution.py:378
  95.4 0.1 shard_map.124
  95.5 10.8 %all_to_all.33.hidden_ref = bf16[16,8,1152]{2,1,0:T(8,128)(2,1)S(1)} all-to-all(bf16[16,8,1152]{2,1,0:T(8,128)(2,1)S(1)} %shard_map.124), channel_id=1, replica_groups={{0,16,32,48,64,80,96,112,128,144,160,176,192,208,224,240},{8,24,40,56,7..., dimensions={0} | all-to-all | bytes 589824 | tf_op jit(solution)/shard_map/all_to_all | solution.py:378
  106.3 3.0 %collective-permute-start.2 = (bf16[16,8,1152]{2,1,0:T(8,128)(2,1)S(1)}, bf16[16,8,1152]{2,1,0:T(8,128)(2,1)S(1)}, u32[]{:S(2)}, u32[]{:S(2)}) collective-permute-start(bf16[16,8,1152]{2,1,0:T(8,128)(2,1)S(1)} %all_to_all.33.hidden_ref), channel_id=1, source_target_pairs={{0,8},{8,0},{16,24},{24,16},{32,40},{40,32},{48,56},{56,48},{64,72... | collective-permute-start | bytes 884744 | tf_op jit(solution)/shard_map/ppermute | solution.py:382
  109.3 0.3 shard_map.125.own_ref
  109.6 0.9 collective-permute-done.2.hidden_ref
  110.5 0.3 shard_map.126
  110.8 9.5 %all_to_all.34.part_ref = bf16[8,16,224]{2,1,0:T(8,128)(2,1)S(1)} all-to-all(bf16[8,16,224]{2,1,0:T(8,128)(2,1)S(1)} %shard_map.126), channel_id=1, replica_groups=mesh['dp'=32,'ctx'=8] {'ctx'}, dimensions={0} | all-to-all | bytes 114688 | tf_op jit(solution)/shard_map/all_to_all | solution.py:372
  120.3 0.6 shard_map.127
  (14 shorter events, 0.0 us)
Async XLA Ops:
  0.0 34.0 %copy-start = (bf16[16,512,128]{2,1,0:T(8,128)(2,1)S(1)}, bf16[16,512,128]{2,1,0:T(8,128)(2,1)}, u32[]{:S(2)}) copy-start(bf16[16,512,128]{2,1,0:T(8,128)(2,1)} %absorb_ref.1) | copy-start | bytes 6291460
  11.1 43.9 %copy-start.4 = (bf16[2048,224]{0,1:T(8,128)(2,1)S(1)}, bf16[2048,224]{0,1:T(8,128)(2,1)}, u32[]{:S(2)}) copy-start(bf16[2048,224]{0,1:T(8,128)(2,1)} %param.19) | copy-start | bytes 2752516
  34.0 22.1 %copy-start.5 = (bf16[16,224]{1,0:T(8,128)(2,1)S(1)}, bf16[16,224]{1,0:T(8,128)(2,1)}, u32[]{:S(2)}) copy-start(bf16[16,224]{1,0:T(8,128)(2,1)} %stream_ref.1) | copy-start | bytes 21508
  53.0 3.1 %collective-permute-start = (bf16[16,8,1024]{2,1,0:T(8,128)(2,1)S(1)}, bf16[16,8,1024]{2,1,0:T(8,128)(2,1)S(1)}, u32[]{:S(2)}, u32[]{:S(2)}) collective-permute-start(bf16[16,8,1024]{2,1,0:T(8,128)(2,1)S(1)} %all_to_all.31.value_ref), channel_id=1, source_target_pairs={{0,8},{8,0},{16,24},{24,16},{32,40},{40,32},{48,56},{56,48},{64,72... | collective-permute-start | bytes 786440 | tf_op jit(solution)/shard_map/ppermute | solution.py:382
  54.9 6.0 %copy-start.6 = (bf16[224]{0:T(256)(128)(2,1)S(1)}, bf16[224]{0:T(256)(128)(2,1)}, u32[]{:S(2)}) copy-start(bf16[224]{0:T(256)(128)(2,1)} %param.20) | copy-start | bytes 1348
  54.9 22.5 %copy-start.2 = (bf16[224,2304]{1,0:T(8,128)(2,1)S(1)}, bf16[224,2304]{1,0:T(8,128)(2,1)}, u32[]{:S(2)}) copy-start(bf16[224,2304]{1,0:T(8,128)(2,1)} %gate_ref.1) | copy-start | bytes 3096580
  54.9 22.5 %copy-start.3 = (bf16[224,2304]{1,0:T(8,128)(2,1)S(1)}, bf16[224,2304]{1,0:T(8,128)(2,1)}, u32[]{:S(2)}) copy-start(bf16[224,2304]{1,0:T(8,128)(2,1)} %up_ref.1) | copy-start | bytes 3096580
  57.5 20.0 %all-to-all-start.2 = ((bf16[8,224,128]{2,1,0:T(8,128)(2,1)}), bf16[8,224,128]{2,1,0:T(8,128)(2,1)S(1)}, u32[]{:S(2)}, u32[]{:S(2)}) async-start(bf16[8,224,128]{2,1,0:T(8,128)(2,1)} %shard_map.121), calls=%async_computation.2 | async-start | bytes 917504 | tf_op jit(solution)/shard_map/all_to_all | solution.py:372
  78.1 2.2 %collective-permute-start.1 = (bf16[16,8,2432]{2,1,0:T(8,128)(2,1)S(1)}, bf16[16,8,2432]{2,1,0:T(8,128)(2,1)S(1)}, u32[]{:S(2)}, u32[]{:S(2)}) collective-permute-start(bf16[16,8,2432]{2,1,0:T(8,128)(2,1)S(1)} %get-tuple-element.9), channel_id=1, source_target_pairs={{0,8},{8,0},{16,24},{24,16},{32,40},{40,32},{48,56},{56,48},{64,72... | collective-permute-start | bytes 1867784 | tf_op jit(solution)/shard_map/ppermute | solution.py:382
  80.3 29.0 %copy-start.1 = (bf16[2304,224]{0,1:T(8,128)(2,1)S(1)}, bf16[2304,224]{0,1:T(8,128)(2,1)}, u32[]{:S(2)}) copy-start(bf16[2304,224]{0,1:T(8,128)(2,1)} %param.23) | copy-start | bytes 3096580
  106.3 4.2 %collective-permute-start.2 = (bf16[16,8,1152]{2,1,0:T(8,128)(2,1)S(1)}, bf16[16,8,1152]{2,1,0:T(8,128)(2,1)S(1)}, u32[]{:S(2)}, u32[]{:S(2)}) collective-permute-start(bf16[16,8,1152]{2,1,0:T(8,128)(2,1)S(1)} %all_to_all.33.hidden_ref), channel_id=1, source_target_pairs={{0,8},{8,0},{16,24},{24,16},{32,40},{40,32},{48,56},{56,48},{64,72... | collective-permute-start | bytes 884744 | tf_op jit(solution)/shard_map/ppermute | solution.py:382

commit v5 on v4

--- a/solution.py
+++ b/solution.py
@@ -292,11 +292,21 @@
     out_ref[...] = jnp.broadcast_to(ordered[None], out_ref.shape)
 
 
-def gate_kernel(part_ref, gain_ref, gate_ref, up_ref, send_ref, keep_ref, mid_ref, whole):
+def gate_products(x, gate_ref, up_ref, k, marks, to_ref):
+    chips, eight, _ = to_ref.shape
+    half = gate_ref.shape[1] // 2
+    columns = pl.ds(pl.multiple_of(k * half, META), half)
+    for i, weight in enumerate((gate_ref, up_ref)):
+        y = jnp.dot(x, weight[:, columns], preferred_element_type=jnp.float32)
+        to_ref[:, :, i * half : (i + 1) * half] = y.reshape(chips, eight, half).astype(to_ref.dtype)
+    to_ref[:, :, 2 * half :] = marks.reshape(chips, eight, META).astype(to_ref.dtype)
+
+
+def gate_kernel(
+    part_ref, gain_ref, gate_ref, up_ref, send_ref, x_ref, marks_ref, mid_ref, whole
+):
     sources, cols, tokens = part_ref.shape
     owned = mid_ref.shape[0]
-    chips, eight, width = send_ref.shape
-    half = gate_ref.shape[1] // 2
     mid = part_ref[0].astype(jnp.float32)
     for c in range(1, sources):
         mid = mid + part_ref[c].astype(jnp.float32)
@@ -307,20 +317,15 @@
     squares = pieces(jnp.sum(mid * mid, axis=1, keepdims=True))
     none = (jnp.zeros_like(squares[0]),) * 3
     x = (mid * gain_ref[...].astype(jnp.float32)).astype(jnp.bfloat16)
+    x_ref[...] = x
+    marks_ref[...] = in_lanes(none + squares, tokens)
     core = lax.axis_index("dp") % 2
-    for to_ref, k, marks in (
-        (send_ref, 1 - core, squares),
-        (keep_ref, core, none + squares),
-    ):
-        for i, weight in enumerate((gate_ref, up_ref)):
-            columns = pl.ds(pl.multiple_of(k * half, META), half)
-            y = jnp.dot(x, weight[:, columns], preferred_element_type=jnp.float32)
-            to_ref[:, :, i * half : (i + 1) * half] = y.reshape(chips, eight, half).astype(
-                to_ref.dtype
-            )
-        to_ref[:, :, 2 * half :] = (
-            in_lanes(marks, tokens).reshape(chips, eight, META).astype(to_ref.dtype)
-        )
+    gate_products(x, gate_ref, up_ref, 1 - core, in_lanes(squares, tokens), send_ref)
+
+
+def gate_own_kernel(x_ref, marks_ref, gate_ref, up_ref, keep_ref):
+    core = lax.axis_index("dp") % 2
+    gate_products(x_ref[...], gate_ref, up_ref, core, marks_ref[...], keep_ref)
 
 
 def pair_kernel(keep_ref, got_ref, out_ref):
@@ -449,20 +454,26 @@
         jax.ShapeDtypeStruct((groups, cols, tokens), bf16),
         vmem(4),
     )(attn, other, out_proj.T, stream)
+    attn, gain = lax.optimization_barrier((attn, norm_gain.reshape(1, cols)))
     attn = exchange(attn, "ctx")
 
     block = (chips, tokens // chips, units + META)
-    send, keep, mid = call(
+    send, x, marks, mid = call(
         gate_kernel,
         (
             jax.ShapeDtypeStruct(block, bf16),
-            jax.ShapeDtypeStruct(block, f32),
+            jax.ShapeDtypeStruct((tokens, cols), bf16),
+            jax.ShapeDtypeStruct((tokens, META), f32),
             jax.ShapeDtypeStruct(stream.shape, bf16),
         ),
         vmem(4),
         [pltpu.VMEM((tokens, cols), f32)],
-    )(attn, norm_gain.reshape(1, cols), gate_weight, up_weight)
-    both = call(pair_kernel, jax.ShapeDtypeStruct(block, bf16), vmem(2))(keep, other_core(send))
+    )(attn, gain, gate_weight, up_weight)
+    got = other_core(send)
+    keep = call(gate_own_kernel, jax.ShapeDtypeStruct(block, f32), vmem(4), cost=work)(
+        x, marks, gate_weight, up_weight
+    )
+    both = call(pair_kernel, jax.ShapeDtypeStruct(block, bf16), vmem(2))(keep, got)
     both = exchange_chips(both)
 
     hidden = call(

time: 121 us -> 119 us (0.983)
  blocking collectives: 76.1 us -> 94.4 us
  waiting for transfers between devices: 19.7 us -> 2.85 us
  starting transfers between devices: 8.92 us -> 5.3 us
    all_to_all x2 -> x3, blocking collectives: 32.5 us -> 55.1 us  [exchange(): return lax.all_to_all(x, axis, 0, 0)]
    all_to_all x1 -> x0, waiting for transfers between devices: 16.5 us -> none  [exchange(): return lax.all_to_all(x, axis, 0, 0)]
    all_to_all x3, blocking collectives: 43.6 us -> 39.3 us  [exchange_chips(): return lax.all_to_all(x, 'dp', 0, 0, axis_index_groups=groups)]
    all_to_all x1 -> x0, starting transfers between devices: 3.47 us -> none  [exchange(): return lax.all_to_all(x, axis, 0, 0)]
  transfers between devices with their start and end apart: 4 -> 3, of which waited for: 4 -> 3; matrix products, arithmetic and copies ran while one was open for 0% -> 0% of each run, Pallas kernels for 1% -> 1%
where the time goes in v5:
time: 119 us; the launch traced here: 118 us
  blocking collectives  94.4 us (79%)
  Pallas kernels  15.5 us (13%)
  starting transfers between devices  5.3 us (4%)
  waiting for transfers between devices  2.85 us (2%)
    all_to_all x3, blocking collectives, exchange(): return lax.all_to_all(x, axis, 0, 0)  55.1 us
    all_to_all x3, blocking collectives, exchange_chips(): return lax.all_to_all(x, 'dp', 0, 0, axis_index_groups=groups)  39.3 us
    pallas_call x1, Pallas kernels, on_device(): call(functools.partial(attend_kernel, sub=512, cuts=cuts), jax.ShapeDtype...  11 us
    ppermute x3, starting transfers between devices, other_core(): lax.ppermute(x, 'dp', [(i, i ^ 1) for i in range(lax.axis_size('dp'))])  5.3 us
    ppermute x3, waiting for transfers between devices, other_core(): lax.ppermute(x, 'dp', [(i, i ^ 1) for i in range(lax.axis_size('dp'))])  2.85 us
  transfers between devices with their start and end apart: 3, of which 3 were waited for; matrix products, arithmetic and copies ran while one was open for 0% of the time, Pallas kernels for 1%

profile of v5, /device:TPU:1, one launch (start us, length us, event | category | flops | bytes accessed | tf_op | source)
XLA Modules:
  0.0 118.2 jit_solution(7541789078424190522)
XLA Ops:
  0.0 11.0 %shard_map.118 = bf16[8,72,512]{2,1,0:T(8,128)(2,1)} custom-call(s32[2]{0:T(128)} %lengths_ref.1, bf16[2,2,576,128]{3,2,1,0:T(8,128)(2,1)} %bitcast.9, bf16[2,2,576]{2,1,0:T(2,128)(2,1)} %new_hbm.1, f32[2,4096]{1,0:T(2,128)} %scale_hbm.1, bf16[2,576,4096]{2,1,0:T(8,128)(2,1)} %bitcast.8), custom_call_target="tpu_custom_call" | custom-call | tf_op jit(solution)/shard_map/pallas_call | solution.py:420
  11.1 26.7 %all_to_all.30.part_ref = bf16[8,72,512]{2,1,0:T(8,128)(2,1)S(1)} all-to-all(bf16[8,72,512]{2,1,0:T(8,128)(2,1)} %shard_map.118), channel_id=1, replica_groups=mesh['dp'=32,'ctx'=8] {'ctx'}, dimensions={0} | all-to-all | bytes 1179648 | tf_op jit(solution)/shard_map/all_to_all | solution.py:377
  37.7 1.1 shard_map.119
  38.8 13.7 %all_to_all.31.value_ref = bf16[16,8,1024]{2,1,0:T(8,128)(2,1)S(1)} all-to-all(bf16[16,8,1024]{2,1,0:T(8,128)(2,1)S(1)} %shard_map.119), channel_id=1, replica_groups={{0,16,32,48,64,80,96,112,128,144,160,176,192,208,224,240},{8,24,40,56,7..., dimensions={0} | all-to-all | bytes 524288 | tf_op jit(solution)/shard_map/all_to_all | solution.py:383
  52.5 1.8 %collective-permute-start = (bf16[16,8,1024]{2,1,0:T(8,128)(2,1)S(1)}, bf16[16,8,1024]{2,1,0:T(8,128)(2,1)S(1)}, u32[]{:S(2)}, u32[]{:S(2)}) collective-permute-start(bf16[16,8,1024]{2,1,0:T(8,128)(2,1)S(1)} %all_to_all.31.value_ref), channel_id=1, source_target_pairs={{0,8},{8,0},{16,24},{24,16},{32,40},{40,32},{48,56},{56,48},{64,72... | collective-permute-start | bytes 786440 | tf_op jit(solution)/shard_map/ppermute | solution.py:387
  54.3 0.0 copy-start
  54.4 0.5 shard_map.120.own_ref
  54.8 0.7 collective-permute-done.value_ref
  55.5 0.6 shard_map.121
  56.1 19.0 %all_to_all.32.part_ref = bf16[8,224,128]{2,1,0:T(8,128)(2,1)S(1)} all-to-all(bf16[8,224,128]{2,1,0:T(8,128)(2,1)S(1)} %shard_map.121), channel_id=1, replica_groups=mesh['dp'=32,'ctx'=8] {'ctx'}, dimensions={0} | all-to-all | bytes 917504 | tf_op jit(solution)/shard_map/all_to_all | solution.py:377
  75.1 0.4 shard_map.122
  75.5 0.6 collective-permute-start.1
  76.1 0.3 shard_map.123.keep_ref
  76.4 1.3 %collective-permute-done.1.got_ref = bf16[16,8,2432]{2,1,0:T(8,128)(2,1)S(1)} collective-permute-done((bf16[16,8,2432]{2,1,0:T(8,128)(2,1)S(1)}, bf16[16,8,2432]{2,1,0:T(8,128)(2,1)S(1)}, u32[]{:S(2)}, u32[]{:S(2)}) %collective-permute-start.1) | collective-permute-done | bytes 622624 | tf_op jit(solution)/shard_map/ppermute | solution.py:387
  77.7 0.1 shard_map.124
  77.8 14.9 %all_to_all.33.part_ref = bf16[16,8,2432]{2,1,0:T(8,128)(2,1)S(1)} all-to-all(bf16[16,8,2432]{2,1,0:T(8,128)(2,1)S(1)} %shard_map.124), channel_id=1, replica_groups={{0,16,32,48,64,80,96,112,128,144,160,176,192,208,224,240},{8,24,40,56,7..., dimensions={0} | all-to-all | bytes 1245184 | tf_op jit(solution)/shard_map/all_to_all | solution.py:383
  92.7 0.1 shard_map.125
  92.8 10.8 %all_to_all.34.hidden_ref = bf16[16,8,1152]{2,1,0:T(8,128)(2,1)S(1)} all-to-all(bf16[16,8,1152]{2,1,0:T(8,128)(2,1)S(1)} %shard_map.125), channel_id=1, replica_groups={{0,16,32,48,64,80,96,112,128,144,160,176,192,208,224,240},{8,24,40,56,7..., dimensions={0} | all-to-all | bytes 589824 | tf_op jit(solution)/shard_map/all_to_all | solution.py:383
  103.6 3.0 %collective-permute-start.2 = (bf16[16,8,1152]{2,1,0:T(8,128)(2,1)S(1)}, bf16[16,8,1152]{2,1,0:T(8,128)(2,1)S(1)}, u32[]{:S(2)}, u32[]{:S(2)}) collective-permute-start(bf16[16,8,1152]{2,1,0:T(8,128)(2,1)S(1)} %all_to_all.34.hidden_ref), channel_id=1, source_target_pairs={{0,8},{8,0},{16,24},{24,16},{32,40},{40,32},{48,56},{56,48},{64,72... | collective-permute-start | bytes 884744 | tf_op jit(solution)/shard_map/ppermute | solution.py:387
  106.6 0.3 shard_map.126.own_ref
  106.9 0.9 collective-permute-done.2.hidden_ref
  107.8 0.3 shard_map.127
  108.1 9.5 %all_to_all.35.part_ref = bf16[8,16,224]{2,1,0:T(8,128)(2,1)S(1)} all-to-all(bf16[8,16,224]{2,1,0:T(8,128)(2,1)S(1)} %shard_map.127), channel_id=1, replica_groups=mesh['dp'=32,'ctx'=8] {'ctx'}, dimensions={0} | all-to-all | bytes 114688 | tf_op jit(solution)/shard_map/all_to_all | solution.py:377
  117.6 0.6 shard_map.128
  (14 shorter events, 0.0 us)
Async XLA Ops:
  0.0 37.7 %copy-start.2 = (bf16[16,512,128]{2,1,0:T(8,128)(2,1)S(1)}, bf16[16,512,128]{2,1,0:T(8,128)(2,1)}, u32[]{:S(2)}) copy-start(bf16[16,512,128]{2,1,0:T(8,128)(2,1)} %absorb_ref.1) | copy-start | bytes 6291460
  11.1 43.3 %copy-start.6 = (bf16[224]{0:T(256)(128)(2,1)S(1)}, bf16[224]{0:T(256)(128)(2,1)}, u32[]{:S(2)}) copy-start(bf16[224]{0:T(256)(128)(2,1)} %param.20) | copy-start | bytes 1348
  11.1 43.3 %copy-start.4 = (bf16[2048,224]{0,1:T(8,128)(2,1)S(1)}, bf16[2048,224]{0,1:T(8,128)(2,1)}, u32[]{:S(2)}) copy-start(bf16[2048,224]{0,1:T(8,128)(2,1)} %param.19) | copy-start | bytes 2752516
  37.7 17.7 %copy-start.5 = (bf16[16,224]{1,0:T(8,128)(2,1)S(1)}, bf16[16,224]{1,0:T(8,128)(2,1)}, u32[]{:S(2)}) copy-start(bf16[16,224]{1,0:T(8,128)(2,1)} %stream_ref.1) | copy-start | bytes 21508
  52.5 2.9 %collective-permute-start = (bf16[16,8,1024]{2,1,0:T(8,128)(2,1)S(1)}, bf16[16,8,1024]{2,1,0:T(8,128)(2,1)S(1)}, u32[]{:S(2)}, u32[]{:S(2)}) collective-permute-start(bf16[16,8,1024]{2,1,0:T(8,128)(2,1)S(1)} %all_to_all.31.value_ref), channel_id=1, source_target_pairs={{0,8},{8,0},{16,24},{24,16},{32,40},{40,32},{48,56},{56,48},{64,72... | collective-permute-start | bytes 786440 | tf_op jit(solution)/shard_map/ppermute | solution.py:387
  54.3 20.7 %copy-start = (bf16[224,2304]{1,0:T(8,128)(2,1)S(1)}, bf16[224,2304]{1,0:T(8,128)(2,1)}, u32[]{:S(2)}) copy-start(bf16[224,2304]{1,0:T(8,128)(2,1)} %gate_ref.3) | copy-start | bytes 3096580
  54.3 20.7 %copy-start.1 = (bf16[224,2304]{1,0:T(8,128)(2,1)S(1)}, bf16[224,2304]{1,0:T(8,128)(2,1)}, u32[]{:S(2)}) copy-start(bf16[224,2304]{1,0:T(8,128)(2,1)} %up_ref.3) | copy-start | bytes 3096580
  75.5 2.2 %collective-permute-start.1 = (bf16[16,8,2432]{2,1,0:T(8,128)(2,1)S(1)}, bf16[16,8,2432]{2,1,0:T(8,128)(2,1)S(1)}, u32[]{:S(2)}, u32[]{:S(2)}) collective-permute-start(bf16[16,8,2432]{2,1,0:T(8,128)(2,1)S(1)} %get-tuple-element.15), channel_id=1, source_target_pairs={{0,8},{8,0},{16,24},{24,16},{32,40},{40,32},{48,56},{56,48},{64,72... | collective-permute-start | bytes 1867784 | tf_op jit(solution)/shard_map/ppermute | solution.py:387
  76.4 30.2 %copy-start.3 = (bf16[2304,224]{0,1:T(8,128)(2,1)S(1)}, bf16[2304,224]{0,1:T(8,128)(2,1)}, u32[]{:S(2)}) copy-start(bf16[2304,224]{0,1:T(8,128)(2,1)} %param.23) | copy-start | bytes 3096580
  103.6 4.2 %collective-permute-start.2 = (bf16[16,8,1152]{2,1,0:T(8,128)(2,1)S(1)}, bf16[16,8,1152]{2,1,0:T(8,128)(2,1)S(1)}, u32[]{:S(2)}, u32[]{:S(2)}) collective-permute-start(bf16[16,8,1152]{2,1,0:T(8,128)(2,1)S(1)} %all_to_all.34.hidden_ref), channel_id=1, source_target_pairs={{0,8},{8,0},{16,24},{24,16},{32,40},{40,32},{48,56},{56,48},{64,72... | collective-permute-start | bytes 884744 | tf_op jit(solution)/shard_map/ppermute | solution.py:387

commit v6 on v5

--- a/solution.py
+++ b/solution.py
@@ -23,9 +23,10 @@
     return [pl.BlockSpec(memory_space=pltpu.VMEM)] * n
 
 
-def call(kernel, out_shape, in_specs, scratch=(), mib=14, cost=None):
+def call(kernel, out_shape, in_specs, scratch=(), mib=14, cost=None, out_specs=None):
     n_out = len(out_shape) if isinstance(out_shape, tuple) else 1
-    out_specs = tuple(vmem(n_out)) if isinstance(out_shape, tuple) else vmem(1)[0]
+    if out_specs is None:
+        out_specs = tuple(vmem(n_out)) if isinstance(out_shape, tuple) else vmem(1)[0]
     return pl.pallas_call(
         kernel,
         in_specs=in_specs,
@@ -58,6 +59,7 @@
     new_hbm,
     scale_hbm,
     cache_hbm,
+    out_hbm,
     out_ref,
     keys,
     scores,
@@ -66,6 +68,7 @@
     scale_ref,
     cache_sems,
     sems,
+    out_sems,
     *,
     sub,
     cuts,
@@ -92,6 +95,14 @@
         pltpu.make_async_copy(scale_hbm, scale_ref, sems.at[2]),
     ]
 
+    early = steps * owned
+    rest = out_ref.shape[1] - early
+    leave = [
+        pltpu.make_async_copy(
+            out_ref.at[:, pl.ds(at, size), :], out_hbm.at[:, pl.ds(at, size), :], out_sems.at[i]
+        )
+        for i, (at, size) in enumerate(((0, early), (early, rest)))
+    ]
     left = [lengths_ref[r] - ctx_id * span for r in range(reqs)]
     queries, fresh, new, tops, totals, sums = ([None] * reqs for _ in range(6))
     n = lax.broadcasted_iota(jnp.int32, (META, width), 0)
@@ -170,11 +181,14 @@
                     weigh(active[n - 1], u)
             if n > 0:
                 write(active[n - 1])
+            if n == 1 and len(active) == reqs:
+                leave[0].start()
             if n < len(active):
                 top(active[n])
         for r in range(reqs):
             if r not in active:
                 skip(r)
+        finish(len(active) < reqs)
 
     def skip(r):
         tops[r] = jnp.full((rows, 1), FLOOR, jnp.float32)
@@ -182,6 +196,13 @@
         sums[r] = jnp.zeros((rows, LATENT), jnp.float32)
         write(r)
 
+    def finish(whole):
+        if whole:
+            leave[0].start()
+        leave[1].start()
+        for copy in leave:
+            copy.wait()
+
     first, second = (left[r] > 0 for r in range(reqs))
 
     @pl.when(first & second)
@@ -200,6 +221,7 @@
     def _():
         for r in range(reqs):
             skip(r)
+        finish(True)
 
 
 def value_kernel(part_ref, absorb_ref, out_ref, marks):
@@ -422,6 +444,7 @@
         jax.ShapeDtypeStruct((groups, reqs * steps * owned + 8, LATENT), bf16),
         [smem] + [pl.BlockSpec(memory_space=pltpu.HBM)] * 4,
         [
+            pltpu.VMEM((groups, reqs * steps * owned + 8, LATENT), bf16),
             pltpu.VMEM((reqs, width, span), bf16),
             pltpu.VMEM((reqs, steps * heads, span), f32),
             pltpu.VMEM((steps, reqs, width, heads), bf16),
@@ -429,8 +452,10 @@
             pltpu.VMEM((reqs, span), f32),
             pltpu.SemaphoreType.DMA((reqs, cuts)),
             pltpu.SemaphoreType.DMA((3,)),
+            pltpu.SemaphoreType.DMA((2,)),
         ],
         mib=56,
+        out_specs=pl.BlockSpec(memory_space=pltpu.HBM),
     )(lengths, query.transpose(0, 1, 3, 2), new_latent, cache_scale, cache.transpose(0, 2, 1))
     part = exchange(part, "ctx")
 

time: 119 us -> 120 us (level)
  starting transfers between devices: 5.3 us -> 7.33 us
    all_to_all x3, blocking collectives: 39.3 us -> 42.2 us  [exchange_chips(): return lax.all_to_all(x, 'dp', 0, 0, axis_index_groups=groups)]
    all_to_all x3, blocking collectives: 55.1 us -> 52.4 us  [exchange(): return lax.all_to_all(x, axis, 0, 0)]
    ppermute x3, starting transfers between devices: 5.3 us -> 7.33 us  [other_core(): lax.ppermute(x, 'dp', [(i, i ^ 1) for i in range(lax.axis_size('dp'))])]
where the time goes in v6:
time: 120 us
  blocking collectives  94.6 us (79%)
  Pallas kernels  15.3 us (13%)
  starting transfers between devices  7.33 us (6%)
  waiting for transfers between devices  2.84 us (2%)
    all_to_all x3, blocking collectives, exchange(): return lax.all_to_all(x, axis, 0, 0)  52.4 us
    all_to_all x3, blocking collectives, exchange_chips(): return lax.all_to_all(x, 'dp', 0, 0, axis_index_groups=groups)  42.2 us
    pallas_call x1, Pallas kernels, on_device(): call(functools.partial(attend_kernel, sub=512, cuts=cuts), jax.ShapeDtype...  10.8 us
    ppermute x3, starting transfers between devices, other_core(): lax.ppermute(x, 'dp', [(i, i ^ 1) for i in range(lax.axis_size('dp'))])  7.33 us
    ppermute x3, waiting for transfers between devices, other_core(): lax.ppermute(x, 'dp', [(i, i ^ 1) for i in range(lax.axis_size('dp'))])  2.84 us
  transfers between devices with their start and end apart: 3, of which 3 were waited for; matrix products, arithmetic and copies ran while one was open for 0% of the time, Pallas kernels for 1%

profile of v6, /device:TPU:1, one launch (start us, length us, event | category | flops | bytes accessed | tf_op | source)
XLA Modules:
  0.0 120.2 jit_solution(9822031391582341980)
XLA Ops:
  0.0 10.8 %shard_map.118 = bf16[8,72,512]{2,1,0:T(8,128)(2,1)} custom-call(s32[2]{0:T(128)} %lengths_ref.1, bf16[2,2,576,128]{3,2,1,0:T(8,128)(2,1)} %bitcast.9, bf16[2,2,576]{2,1,0:T(2,128)(2,1)} %new_hbm.1, f32[2,4096]{1,0:T(2,128)} %scale_hbm.1, bf16[2,576,4096]{2,1,0:T(8,128)(2,1)} %bitcast.8), custom_call_target="tpu_custom_call" | custom-call | tf_op jit(solution)/shard_map/pallas_call | solution.py:442
  10.8 0.0 copy-start.6
  10.8 24.0 %all_to_all.30.part_ref = bf16[8,72,512]{2,1,0:T(8,128)(2,1)S(1)} all-to-all(bf16[8,72,512]{2,1,0:T(8,128)(2,1)} %shard_map.118), channel_id=1, replica_groups=mesh['dp'=32,'ctx'=8] {'ctx'}, dimensions={0} | all-to-all | bytes 1179648 | tf_op jit(solution)/shard_map/all_to_all | solution.py:399
  34.8 1.1 shard_map.119
  35.9 16.5 %all_to_all.31.value_ref = bf16[16,8,1024]{2,1,0:T(8,128)(2,1)S(1)} all-to-all(bf16[16,8,1024]{2,1,0:T(8,128)(2,1)S(1)} %shard_map.119), channel_id=1, replica_groups={{0,16,32,48,64,80,96,112,128,144,160,176,192,208,224,240},{8,24,40,56,7..., dimensions={0} | all-to-all | bytes 524288 | tf_op jit(solution)/shard_map/all_to_all | solution.py:405
  52.4 3.8 %collective-permute-start = (bf16[16,8,1024]{2,1,0:T(8,128)(2,1)S(1)}, bf16[16,8,1024]{2,1,0:T(8,128)(2,1)S(1)}, u32[]{:S(2)}, u32[]{:S(2)}) collective-permute-start(bf16[16,8,1024]{2,1,0:T(8,128)(2,1)S(1)} %all_to_all.31.value_ref), channel_id=1, source_target_pairs={{0,8},{8,0},{16,24},{24,16},{32,40},{40,32},{48,56},{56,48},{64,72... | collective-permute-start | bytes 786440 | tf_op jit(solution)/shard_map/ppermute | solution.py:409
  56.3 0.5 shard_map.120.own_ref
  56.8 0.6 collective-permute-done.value_ref
  57.4 0.6 shard_map.121
  58.0 19.0 %all_to_all.32.part_ref = bf16[8,224,128]{2,1,0:T(8,128)(2,1)S(1)} all-to-all(bf16[8,224,128]{2,1,0:T(8,128)(2,1)S(1)} %shard_map.121), channel_id=1, replica_groups=mesh['dp'=32,'ctx'=8] {'ctx'}, dimensions={0} | all-to-all | bytes 917504 | tf_op jit(solution)/shard_map/all_to_all | solution.py:399
  77.0 0.4 shard_map.122
  77.4 0.6 collective-permute-start.1
  78.0 0.3 shard_map.123.keep_ref
  78.4 1.3 %collective-permute-done.1.got_ref = bf16[16,8,2432]{2,1,0:T(8,128)(2,1)S(1)} collective-permute-done((bf16[16,8,2432]{2,1,0:T(8,128)(2,1)S(1)}, bf16[16,8,2432]{2,1,0:T(8,128)(2,1)S(1)}, u32[]{:S(2)}, u32[]{:S(2)}) %collective-permute-start.1) | collective-permute-done | bytes 622624 | tf_op jit(solution)/shard_map/ppermute | solution.py:409
  79.7 0.1 shard_map.124
  79.8 14.9 %all_to_all.33.part_ref = bf16[16,8,2432]{2,1,0:T(8,128)(2,1)S(1)} all-to-all(bf16[16,8,2432]{2,1,0:T(8,128)(2,1)S(1)} %shard_map.124), channel_id=1, replica_groups={{0,16,32,48,64,80,96,112,128,144,160,176,192,208,224,240},{8,24,40,56,7..., dimensions={0} | all-to-all | bytes 1245184 | tf_op jit(solution)/shard_map/all_to_all | solution.py:405
  94.7 0.1 shard_map.125
  94.8 10.8 %all_to_all.34.hidden_ref = bf16[16,8,1152]{2,1,0:T(8,128)(2,1)S(1)} all-to-all(bf16[16,8,1152]{2,1,0:T(8,128)(2,1)S(1)} %shard_map.125), channel_id=1, replica_groups={{0,16,32,48,64,80,96,112,128,144,160,176,192,208,224,240},{8,24,40,56,7..., dimensions={0} | all-to-all | bytes 589824 | tf_op jit(solution)/shard_map/all_to_all | solution.py:405
  105.6 3.0 %collective-permute-start.2 = (bf16[16,8,1152]{2,1,0:T(8,128)(2,1)S(1)}, bf16[16,8,1152]{2,1,0:T(8,128)(2,1)S(1)}, u32[]{:S(2)}, u32[]{:S(2)}) collective-permute-start(bf16[16,8,1152]{2,1,0:T(8,128)(2,1)S(1)} %all_to_all.34.hidden_ref), channel_id=1, source_target_pairs={{0,8},{8,0},{16,24},{24,16},{32,40},{40,32},{48,56},{56,48},{64,72... | collective-permute-start | bytes 884744 | tf_op jit(solution)/shard_map/ppermute | solution.py:409
  108.5 0.3 shard_map.126.own_ref
  108.9 0.9 collective-permute-done.2.hidden_ref
  109.8 0.3 shard_map.127
  110.1 9.5 %all_to_all.35.part_ref = bf16[8,16,224]{2,1,0:T(8,128)(2,1)S(1)} all-to-all(bf16[8,16,224]{2,1,0:T(8,128)(2,1)S(1)} %shard_map.127), channel_id=1, replica_groups=mesh['dp'=32,'ctx'=8] {'ctx'}, dimensions={0} | all-to-all | bytes 114688 | tf_op jit(solution)/shard_map/all_to_all | solution.py:399
  119.6 0.6 shard_map.128
  (14 shorter events, 0.0 us)
Async XLA Ops:
  0.0 34.8 %copy-start.2 = (bf16[16,512,128]{2,1,0:T(8,128)(2,1)S(1)}, bf16[16,512,128]{2,1,0:T(8,128)(2,1)}, u32[]{:S(2)}) copy-start(bf16[16,512,128]{2,1,0:T(8,128)(2,1)} %absorb_ref.1) | copy-start | bytes 6291460
  10.8 45.4 %copy-start.6 = (bf16[224]{0:T(256)(128)(2,1)S(1)}, bf16[224]{0:T(256)(128)(2,1)}, u32[]{:S(2)}) copy-start(bf16[224]{0:T(256)(128)(2,1)} %param.20) | copy-start | bytes 1348
  10.8 45.4 %copy-start.4 = (bf16[2048,224]{0,1:T(8,128)(2,1)S(1)}, bf16[2048,224]{0,1:T(8,128)(2,1)}, u32[]{:S(2)}) copy-start(bf16[2048,224]{0,1:T(8,128)(2,1)} %param.19) | copy-start | bytes 2752516
  34.8 22.6 %copy-start.5 = (bf16[16,224]{1,0:T(8,128)(2,1)S(1)}, bf16[16,224]{1,0:T(8,128)(2,1)}, u32[]{:S(2)}) copy-start(bf16[16,224]{1,0:T(8,128)(2,1)} %stream_ref.1) | copy-start | bytes 21508
  52.4 5.0 %collective-permute-start = (bf16[16,8,1024]{2,1,0:T(8,128)(2,1)S(1)}, bf16[16,8,1024]{2,1,0:T(8,128)(2,1)S(1)}, u32[]{:S(2)}, u32[]{:S(2)}) collective-permute-start(bf16[16,8,1024]{2,1,0:T(8,128)(2,1)S(1)} %all_to_all.31.value_ref), channel_id=1, source_target_pairs={{0,8},{8,0},{16,24},{24,16},{32,40},{40,32},{48,56},{56,48},{64,72... | collective-permute-start | bytes 786440 | tf_op jit(solution)/shard_map/ppermute | solution.py:409
  56.3 20.7 %copy-start = (bf16[224,2304]{1,0:T(8,128)(2,1)S(1)}, bf16[224,2304]{1,0:T(8,128)(2,1)}, u32[]{:S(2)}) copy-start(bf16[224,2304]{1,0:T(8,128)(2,1)} %gate_ref.3) | copy-start | bytes 3096580
  56.3 20.7 %copy-start.1 = (bf16[224,2304]{1,0:T(8,128)(2,1)S(1)}, bf16[224,2304]{1,0:T(8,128)(2,1)}, u32[]{:S(2)}) copy-start(bf16[224,2304]{1,0:T(8,128)(2,1)} %up_ref.3) | copy-start | bytes 3096580
  77.4 2.2 %collective-permute-start.1 = (bf16[16,8,2432]{2,1,0:T(8,128)(2,1)S(1)}, bf16[16,8,2432]{2,1,0:T(8,128)(2,1)S(1)}, u32[]{:S(2)}, u32[]{:S(2)}) collective-permute-start(bf16[16,8,2432]{2,1,0:T(8,128)(2,1)S(1)} %get-tuple-element.15), channel_id=1, source_target_pairs={{0,8},{8,0},{16,24},{24,16},{32,40},{40,32},{48,56},{56,48},{64,72... | collective-permute-start | bytes 1867784 | tf_op jit(solution)/shard_map/ppermute | solution.py:409
  78.3 30.2 %copy-start.3 = (bf16[2304,224]{0,1:T(8,128)(2,1)S(1)}, bf16[2304,224]{0,1:T(8,128)(2,1)}, u32[]{:S(2)}) copy-start(bf16[2304,224]{0,1:T(8,128)(2,1)} %param.23) | copy-start | bytes 3096580
  105.6 4.2 %collective-permute-start.2 = (bf16[16,8,1152]{2,1,0:T(8,128)(2,1)S(1)}, bf16[16,8,1152]{2,1,0:T(8,128)(2,1)S(1)}, u32[]{:S(2)}, u32[]{:S(2)}) collective-permute-start(bf16[16,8,1152]{2,1,0:T(8,128)(2,1)S(1)} %all_to_all.34.hidden_ref), channel_id=1, source_target_pairs={{0,8},{8,0},{16,24},{24,16},{32,40},{40,32},{48,56},{56,48},{64,72... | collective-permute-start | bytes 884744 | tf_op jit(solution)/shard_map/ppermute | solution.py:409
